TPU v7x, 32 devices: a whole 2x2x4 slice. The times are simulated.
32 devices in a mesh: clu: 8 (over z, y), col: 4 (over x, core).
Axes of the slice: x: 2, y: 2, z: 4, core: 2. Of those that a mesh axis runs over, the one named last changes fastest.
Arguments:
- features: bfloat16 [8192, 2048], P('clu', 'col'), may hold values from -6 to 6
- weight: bfloat16 [2048, 2048], P(None, 'col'), may hold values from -0.125 to 0.125
- layer_bias: bfloat16 [2048], P('col'), may hold values from -3 to 3
- cotangent: bfloat16 [8192, 2048], P('clu', 'col'), may hold values from -24 to 24
- self_weight: float32 [8192], P('clu'), may hold values from 0.1 to 0.4
- local_index: int32 [8192, 16], P('clu'), may hold values from 0 to 1023
- local_weight: float32 [8192, 16], P('clu'), may hold values from 0.1 to 0.4
- send_index: int32 [8, 8, 64], P('clu'), may hold values from -1 to 1023, as said below
- remote_slot: int32 [8192, 8], P('clu'), may hold values from 0 to 511, as said below
- remote_weight: float32 [8192, 8], P('clu'), may hold values from 0.1 to 0.4
Outputs:
- activations: bfloat16 [8192, 2048], P('clu')
- input_grad: bfloat16 [8192, 2048], P('clu', 'col')
- weight_grad: float32 [2048, 2048], P(None, 'col')
- bias_grad: float32 [2048], P('col')
Inputs may be any that keep to these rules, and one draw needn't show every extreme that they name: Entries send_index[s, t, j] for j below a count n(s, t) are row numbers of cluster s read by cluster t; the rest are -1. n(s, s) = 0; otherwise 1 <= n(s, t) <= 64, and every cluster sends 64 rows to one other cluster and receives 64 rows from one other cluster. remote_slot[i, k] = s * 64 + j names a slot j < n(s, t) of a cluster s different from i's cluster t, so it always holds a sent row.
All inputs are finite; a program needn't handle non-finite values.
Results may differ from a plain program's by a relative error of at most 0.015.
Values may be sent and summed in bfloat16 or wider, within the bound.
A program may use at most 128 MiB of HBM per device.

v0:
```python
import functools
import math

import jax
import jax.numpy as jnp
from jax import lax
from jax.experimental import pallas as pl
from jax.experimental.pallas import tpu as pltpu
from jax.sharding import PartitionSpec as P

enhance = 1.0
f32, bf16, i32 = jnp.float32, jnp.bfloat16, jnp.int32
MESH = pl.DeviceIdType.MESH
BLOCKS = 4
HALVES = 2
UNROLL = 8


def tn(a, b):
    return lax.dot_general(a, b, (((0,), (0,)), ((), ())), preferred_element_type=f32)


def nt(a, b):
    return lax.dot_general(a, b, (((1,), (1,)), ((), ())), preferred_element_type=f32)


def nn(a, b):
    return jnp.dot(a, b, preferred_element_type=f32)


def layer(
    feat, weight_in, bias, cot_in, selfw, lidx, lwgt, send, ridx, rwgt,
    act_out, ig_out, wg_out, bg_out,
    w_v, cot_v, sel, near, far, edge_pos, edge_w, outg, incg, wide, merged, act, glow, keep_own, keep_far,
    csend, crecv, xsend, xrecv, gm, wacc, ysend, yrecv, zsend, zrecv, wfin, bsend, brecv, ret,
    load_s, in_s, in_r, tab_s, tab_r, mx_s, mx_r, mc_s, mc_r, mf_s, mf_r, rc_s, rc_r, rx_s, rx_r,
    y_s, y_r, z_s, z_r, zg_s, zg_r, yg_s, yg_r, b_s, b_r, ret_s, ret_r, ax_s, ax_r, ac_s, ac_r, af_s, af_r, out_s,
    *, n, ncol,
):
    rows, part = feat.shape
    half = part // HALVES
    rb = rows // BLOCKS
    slots = send.shape[1]
    gd = min(8, n)
    groups = n // gd
    gs = gd * slots
    depth = n // 2
    kb = wacc.shape[0] // n

    me = lax.axis_index("clu")
    col = lax.axis_index("col")
    zz, yy = lax.div(me, 2), lax.rem(me, 2)
    core = lax.rem(col, 2)
    pair = col + 1 - 2 * core
    xcol = lax.rem(col + ncol // 2, ncol)
    dcol = lax.rem(pair + ncol // 2, ncol)
    ypeer = (me + 1 - 2 * yy, col)
    pending = []

    def put(src, dst, ss, rs, dev):
        copy = pltpu.make_async_remote_copy(
            src_ref=src, dst_ref=dst, send_sem=ss, recv_sem=rs, device_id=dev, device_id_type=MESH
        )
        copy.start()
        pending.append(copy)

    def got(dst, rs):
        pltpu.make_async_remote_copy(
            src_ref=dst, dst_ref=dst, send_sem=rs, recv_sem=rs, device_id=(me, pair), device_id_type=MESH
        ).wait_recv()

    def sent(src, ss):
        pltpu.make_async_remote_copy(
            src_ref=src, dst_ref=src, send_sem=ss, recv_sem=ss, device_id=(me, pair), device_id_type=MESH
        ).wait_send()

    def peers(step):
        def body(k, carry):
            step(lax.rem(me + k, n))
            return carry

        lax.fori_loop(1, n, body, 0)

    load_w = pltpu.make_async_copy(weight_in, w_v, load_s.at[0])
    load_c = pltpu.make_async_copy(cot_in, cot_v, load_s.at[1])
    load_w.start()
    load_c.start()
    barrier = pltpu.get_barrier_semaphore()
    peers(lambda t: pl.semaphore_signal(barrier, inc=1, device_id=(t, col), device_id_type=MESH))
    for other in (pair, xcol):
        pl.semaphore_signal(barrier, inc=1, device_id=(me, other), device_id_type=MESH)

    lane = lax.broadcasted_iota(i32, (slots, rows), 1)

    def put_selector(g):
        ids = send[g * gd : (g + 1) * gd, :].T
        for d in range(gd):
            sel[d * slots : (d + 1) * slots, :] = jnp.where(ids[:, d : d + 1] == lane, 1.0, 0.0).astype(bf16)

    def in_copy(h, t):
        pltpu.make_async_remote_copy(
            src_ref=outg.at[h, t], dst_ref=incg.at[h, me], send_sem=in_s.at[h, t], recv_sem=in_r.at[h, me],
            device_id=(t, col), device_id_type=MESH,
        ).start()

    for h in range(HALVES):
        for g in range(groups):
            if groups > 1 or h == 0:
                put_selector(g)
            rows_out = nn(sel[...], feat[:, h * half : (h + 1) * half]).astype(bf16)
            outg[h, g * gd : (g + 1) * gd] = rows_out.reshape(gd, slots, half)
        if h == 0:
            pl.semaphore_wait(barrier, n + 1)
        peers(functools.partial(in_copy, h))
        incg[h, me] = jnp.zeros((slots, half), bf16)

    local_edges, far_edges = lidx.shape[1], ridx.shape[1]
    first_far = local_edges + 1

    def put_edges(at, idx, w):
        for k in range(idx.shape[0]):
            edge_pos[at + k] = jnp.broadcast_to(idx[k : k + 1, :], (8, rows))
            edge_w[at + k] = jnp.broadcast_to(w[k : k + 1, :], (8, rows))

    put_edges(0, lidx[...].T, lwgt[...].T)
    put_edges(local_edges, lax.broadcasted_iota(i32, (1, rows), 1), (1.0 + enhance) * selfw[...])
    put_edges(first_far, ridx[...].T, rwgt[...].T)
    sub = lax.broadcasted_iota(i32, (8, 128), 0)

    def table(dst, first, count, base, edge_from, edge_to):
        tall = 16 * UNROLL

        def lanes(l, carry):
            ls = pl.ds(pl.multiple_of(l * 128, 128), 128)

            def step(b, carry):
                r0 = first + b * tall
                places = [sub + (base + r0 + 8 * u) for u in range(2 * UNROLL)]
                sums = [jnp.zeros((8, 128), f32)] * (2 * UNROLL)
                for k in range(edge_from, edge_to):
                    at, w = edge_pos[k, :, ls], edge_w[k, :, ls]
                    sums = [s + jnp.where(at == p, w, 0.0) for s, p in zip(sums, places)]
                dst[pl.ds(pl.multiple_of(r0, 16), tall), ls] = jnp.concatenate(sums, 0).astype(bf16)
                return carry

            return lax.fori_loop(0, count // tall, step, carry)

        lax.fori_loop(0, rows // 128, lanes, 0)

    def shared_table(dst, which, edge_from, edge_to):
        count = dst.shape[0] // 2
        table(dst, core * count, count, 0, edge_from, edge_to)
        mine = dst.at[pl.ds(pl.multiple_of(core * count, count), count)]
        put(mine, mine, tab_s.at[which], tab_r.at[which], (me, pair))

    def wait_table(dst, which):
        count = dst.shape[0] // 2
        got(dst.at[pl.ds(pl.multiple_of((1 - core) * count, count), count)], tab_r.at[which])

    def far_group(g):
        table(far, 0, gs, g * gs, first_far, first_far + far_edges)

    shared_table(near, 0, 0, first_far)
    if groups == 1:
        shared_table(far, 1, first_far, first_far + far_edges)
    wait_table(near, 0)
    for r in range(BLOCKS):
        rs = slice(r * rb, (r + 1) * rb)
        wide[rs, :] = tn(near[:, rs], feat[...])
    if groups == 1:
        wait_table(far, 1)

    def arrived(h):
        peers(lambda s: got(incg.at[h, s], in_r.at[h, s]))

    def send_merged(h, r):
        piece = merged.at[col, h, pl.ds(r * rb, rb)]
        put(piece, piece, mx_s.at[h, r], mx_r.at[h, r], (me, xcol))
        put(piece, piece, mc_s.at[h, r], mc_r.at[h, r], (me, pair))

    if groups == 1:
        for h in range(HALVES):
            hs = slice(h * half, (h + 1) * half)
            arrived(h)
            pooled = incg[h].reshape(gs, half)
            for r in range(BLOCKS):
                rs = slice(r * rb, (r + 1) * rb)
                merged[col, h, rs] = (wide[rs, hs] + tn(far[:, rs], pooled)).astype(bf16)
                send_merged(h, r)
    else:
        for h in range(HALVES):
            arrived(h)
        for g in range(groups):
            far_group(g)
            for h in range(HALVES):
                hs = slice(h * half, (h + 1) * half)
                pooled = incg[h, g * gd : (g + 1) * gd].reshape(gs, half)
                for r in range(BLOCKS):
                    rs = slice(r * rb, (r + 1) * rb)
                    wide[rs, hs] += tn(far[:, rs], pooled)
        for h in range(HALVES):
            hs = slice(h * half, (h + 1) * half)
            for r in range(BLOCKS):
                rs = slice(r * rb, (r + 1) * rb)
                merged[col, h, rs] = wide[rs, hs].astype(bf16)
                send_merged(h, r)

    load_w.wait()
    load_c.wait()

    def cross(h, r):
        piece = merged.at[xcol, h, pl.ds(r * rb, rb)]
        got(piece, mx_r.at[h, r])
        put(piece, piece, mf_s.at[h, r], mf_r.at[h, r], (me, pair))

    def whole_rows(h, r):
        got(merged.at[pair, h, pl.ds(r * rb, rb)], mc_r.at[h, r])
        got(merged.at[dcol, h, pl.ds(r * rb, rb)], mf_r.at[h, r])

    def products(h, r):
        total = None
        for q in range(ncol):
            k0 = q * part + h * half
            term = nn(merged[q, h, r * rb : (r + 1) * rb, :], w_v[k0 : k0 + half, :])
            total = term if total is None else total + term
        return total

    def first_half(r):
        whole_rows(0, r)
        wide[r * rb : (r + 1) * rb, :] = products(0, r) + bias[...]

    def second_half(r):
        whole_rows(1, r)
        wide[r * rb : (r + 1) * rb, :] += products(1, r)

    tall = 32

    def smooth(r, total):
        def step(b, total):
            rs = pl.ds(pl.multiple_of(r * rb + b * tall, tall), tall)
            v = wide[rs, :]
            cdf = 0.5 + 0.5 * lax.erf(v * (1.0 / math.sqrt(2.0)))
            act[col, rs, :] = (v * cdf).astype(bf16)
            density = jnp.exp(v * v * -0.5) * (1.0 / math.sqrt(2.0 * math.pi))
            low = (cot_v[rs, :].astype(f32) * (cdf + v * density)).astype(bf16)
            glow[rs, :] = low
            return total + jnp.sum(low.astype(f32).reshape(tall // 8, 8, part), axis=0)

        return lax.fori_loop(0, rb // tall, step, total)

    def grads(r):
        rs = slice(r * rb, (r + 1) * rb)
        low = glow[rs, :]

        def term(q):
            return nt(low, w_v[pl.ds(pl.multiple_of(q * part, part), part), :])

        csend[r, 0] = term(pair).astype(bf16)
        csend[r, 1] = term(dcol).astype(bf16)
        put(csend.at[r], crecv.at[r], rc_s.at[r], rc_r.at[r], (me, pair))
        keep_own[rs, :] = term(col)
        keep_far[rs, :] = term(xcol)

    def grads_over(r):
        rs = slice(r * rb, (r + 1) * rb)
        got(crecv.at[r], rc_r.at[r])
        xsend[r] = (keep_far[rs, :] + crecv[r, 1].astype(f32)).astype(bf16)
        put(xsend.at[r], xrecv.at[r], rx_s.at[r], rx_r.at[r], (me, xcol))
        keep_own[rs, :] += crecv[r, 0].astype(f32)

    def grads_in(r):
        rs = slice(r * rb, (r + 1) * rb)
        got(xrecv.at[r], rx_r.at[r])
        gm[rs, :] = (keep_own[rs, :] + xrecv[r].astype(f32)).astype(bf16)

    for r in range(BLOCKS):
        cross(0, r)
        if r:
            first_half(r - 1)
    total = jnp.zeros((8, part), f32)
    for r in range(BLOCKS):
        cross(1, r)
        if r == 0:
            first_half(BLOCKS - 1)
        else:
            grads_over(r - 1)
        second_half(r)
        total = smooth(r, total)
        grads(r)

    bsend[...] = total

    def weight_chunk(chunk):
        q, h = lax.div(chunk, HALVES), lax.rem(chunk, HALVES)
        return tn(merged[q, h], glow[...])

    fine = kb == half
    if not fine:
        for chunk in range(ncol * HALVES):
            wacc[chunk * half : (chunk + 1) * half, :] = tn(merged[chunk // HALVES, chunk % HALVES], glow[...])

    def block_rows(b):
        return pl.ds(pl.multiple_of(b * kb, kb), kb)

    def place(k):
        return lax.rem(zz + k, depth)

    def weight_out(k):
        z = place(k)
        theirs, mine = z * 2 + 1 - yy, z * 2 + yy
        if fine:
            ysend[z] = weight_chunk(theirs).astype(bf16)
        else:
            ysend[z] = wacc[block_rows(theirs), :].astype(bf16)
        put(ysend.at[z], yrecv.at[z], y_s.at[z], y_r.at[z], ypeer)
        if fine:
            wacc[block_rows(mine), :] = weight_chunk(mine)

    def weight_pass(k):
        z = place(k)
        got(yrecv.at[z], y_r.at[z])
        summed = wacc[block_rows(z * 2 + yy), :] + yrecv[z].astype(f32)
        if k:
            zsend[z] = summed.astype(bf16)
            put(zsend.at[z], zrecv.at[zz], z_s.at[z], z_r.at[zz], (z * 2 + yy, col))
        else:
            wacc[block_rows(me), :] = summed

    order = list(range(1, depth)) + [0]
    for at, k in enumerate(order):
        weight_out(k)
        if at == 0:
            grads_over(BLOCKS - 1)

    def bias_copy(t):
        pltpu.make_async_remote_copy(
            src_ref=bsend, dst_ref=brecv.at[me], send_sem=b_s.at[t], recv_sem=b_r.at[me],
            device_id=(t, col), device_id_type=MESH,
        ).start()

    peers(bias_copy)

    def act_over(r):
        piece = act.at[col, pl.ds(r * rb, rb)]
        put(piece, piece, ax_s.at[r], ax_r.at[r], (me, xcol))

    own_act = act.at[col]
    put(own_act, own_act, ac_s.at[0], ac_r.at[0], (me, pair))
    columns = lambda q: pl.ds(pl.multiple_of(q * part, part), part)
    saves = [pltpu.make_async_copy(own_act, act_out.at[:, columns(col)], out_s.at[0])]
    saves[0].start()

    for k in order[: depth - 3]:
        weight_pass(k)
    grads_in(0)
    grads_in(1)
    weight_pass(order[depth - 3])
    grads_in(2)
    act_over(0)
    weight_pass(order[depth - 2])
    grads_in(3)
    for r in range(1, BLOCKS):
        act_over(r)

    def sent_in(h):
        peers(lambda t: sent(outg.at[h, t], in_s.at[h, t]))

    for h in range(HALVES):
        sent_in(h)

    def back_copy(h, t):
        pltpu.make_async_remote_copy(
            src_ref=outg.at[h, t], dst_ref=ret.at[h, me], send_sem=ret_s.at[h, t], recv_sem=ret_r.at[h, me],
            device_id=(t, col), device_id_type=MESH,
        ).start()

    for g in range(groups):
        if groups > 1:
            far_group(g)
        pool_grad = nn(far[...], gm[...]).astype(bf16)
        for h in range(HALVES):
            outg[h, g * gd : (g + 1) * gd] = pool_grad[:, h * half : (h + 1) * half].reshape(gd, slots, half)
    for h in range(HALVES):
        peers(functools.partial(back_copy, h))
        ret[h, me] = jnp.zeros((slots, half), bf16)
    weight_pass(0)
    for r in range(BLOCKS):
        rs = slice(r * rb, (r + 1) * rb)
        wide[rs, :] = nn(near[rs, :], gm[...])

    mine = wacc[block_rows(me), :]
    for k in range(1, depth):
        z = place(k)
        got(zrecv.at[z], z_r.at[z])
        mine = mine + zrecv[z].astype(f32)
    wfin[me] = mine.astype(bf16)
    block = wfin.at[me]
    for k in range(1, depth):
        z = place(k)
        put(block, block, zg_s.at[z], zg_r.at[zz], (z * 2 + yy, col))
    put(block, block, yg_s.at[zz], yg_r.at[zz], ypeer)

    for h in range(HALVES):
        hs = slice(h * half, (h + 1) * half)
        peers(lambda s: got(ret.at[h, s], ret_r.at[h, s]))
        for g in range(groups):
            if groups > 1:
                put_selector(g)
            back = ret[h, g * gd : (g + 1) * gd].reshape(gs, half)
            for r in range(BLOCKS):
                rs = slice(r * rb, (r + 1) * rb)
                wide[rs, hs] += tn(sel[:, rs], back)
        ig_out[:, hs] = wide[:, hs].astype(bf16)

    for k in range(1, depth):
        z = place(k)
        block = wfin.at[z * 2 + yy]
        got(block, zg_r.at[z])
        put(block, block, yg_s.at[z], yg_r.at[z], ypeer)
    for r in range(BLOCKS):
        piece = act.at[xcol, pl.ds(r * rb, rb)]
        got(piece, ax_r.at[r])
        put(piece, piece, af_s.at[r], af_r.at[r], (me, pair))
    got(act.at[pair], ac_r.at[0])
    for at, q in enumerate((pair, xcol)):
        saves.append(pltpu.make_async_copy(act.at[q], act_out.at[:, columns(q)], out_s.at[1 + at]))
        saves[-1].start()
    peers(lambda s: got(brecv.at[s], b_r.at[s]))
    brecv[me] = bsend[...]
    bg_out[...] = jnp.sum(brecv[...].reshape(n * 8, part), axis=0, keepdims=True)
    for r in range(BLOCKS):
        got(act.at[dcol, pl.ds(r * rb, rb)], af_r.at[r])
    saves.append(pltpu.make_async_copy(act.at[dcol], act_out.at[:, columns(dcol)], out_s.at[3]))
    saves[-1].start()
    for k in range(depth):
        z = place(k)
        got(wfin.at[z * 2 + 1 - yy], yg_r.at[z])
    saves.append(pltpu.make_async_copy(wfin, wg_out, out_s.at[4]))
    saves[-1].start()

    peers(lambda t: sent(bsend, b_s.at[t]))
    for h in range(HALVES):
        peers(lambda t: sent(outg.at[h, t], ret_s.at[h, t]))
    for copy in pending:
        copy.wait_send()
    for save in saves:
        save.wait()


def local(
    features, weight, layer_bias, cotangent, self_weight, local_index, local_weight, send_index, remote_slot, remote_weight,
    *, n, ncol,
):
    rows, part = features.shape
    width = weight.shape[0]
    slots = send_index.shape[2]
    half, rb = part // HALVES, rows // BLOCKS
    gs = min(8, n) * slots
    depth, kb = n // 2, width // n
    edges = local_index.shape[1] + 1 + remote_slot.shape[1]
    vmem = pl.BlockSpec(memory_space=pltpu.VMEM)
    hbm = pl.BlockSpec(memory_space=pl.ANY)
    V = pltpu.VMEM
    S = lambda *shape: pltpu.SemaphoreType.DMA(shape)
    buffers = [
        V((width, part), bf16), V((rows, part), bf16), V((gs, rows), bf16), V((rows, rows), bf16), V((gs, rows), bf16),
        V((edges, 8, rows), i32), V((edges, 8, rows), f32),
        V((HALVES, n, slots, half), bf16), V((HALVES, n, slots, half), bf16), V((rows, part), f32),
        V((ncol, HALVES, rows, half), bf16), V((ncol, rows, part), bf16), V((rows, part), bf16),
        V((rows, part), f32), V((rows, part), f32),
        V((BLOCKS, 2, rb, part), bf16), V((BLOCKS, 2, rb, part), bf16), V((BLOCKS, rb, part), bf16), V((BLOCKS, rb, part), bf16),
        V((rows, part), bf16), V((width, part), f32),
        V((depth, kb, part), bf16), V((depth, kb, part), bf16), V((depth, kb, part), bf16), V((depth, kb, part), bf16),
        V((n, kb, part), bf16), V((8, part), f32), V((n, 8, part), f32), V((HALVES, n, slots, half), bf16),
    ]
    semaphores = [
        S(2), S(HALVES, n), S(HALVES, n), S(2), S(2),
        S(HALVES, BLOCKS), S(HALVES, BLOCKS), S(HALVES, BLOCKS), S(HALVES, BLOCKS), S(HALVES, BLOCKS), S(HALVES, BLOCKS),
        S(BLOCKS), S(BLOCKS), S(BLOCKS), S(BLOCKS),
        S(depth), S(depth), S(depth), S(depth), S(depth), S(depth), S(depth), S(depth),
        S(n), S(n), S(HALVES, n), S(HALVES, n),
        S(BLOCKS), S(BLOCKS), S(1), S(1), S(BLOCKS), S(BLOCKS), S(5),
    ]
    act, ig, wg, bg = pl.pallas_call(
        functools.partial(layer, n=n, ncol=ncol),
        out_shape=(
            jax.ShapeDtypeStruct((rows, ncol * part), bf16),
            jax.ShapeDtypeStruct((rows, part), bf16),
            jax.ShapeDtypeStruct((n, kb, part), bf16),
            jax.ShapeDtypeStruct((1, part), f32),
        ),
        in_specs=[vmem, hbm, vmem, hbm, vmem, vmem, vmem, vmem, vmem, vmem],
        out_specs=(hbm, vmem, hbm, vmem),
        scratch_shapes=buffers + semaphores,
        compiler_params=pltpu.CompilerParams(
            collective_id=0, has_side_effects=True, vmem_limit_bytes=62 << 20
        ),
        cost_estimate=pl.CostEstimate(flops=11 << 30, bytes_accessed=16 << 20, transcendentals=1 << 20),
    )(
        features, weight, layer_bias.astype(f32)[None, :], cotangent, self_weight[None, :], local_index, local_weight,
        send_index[0], remote_slot, remote_weight,
    )
    return act, ig, wg.reshape(width, part).astype(f32), bg[0]


def solution(mesh):
    placed = (
        P("clu", "col"),
        P(None, "col"),
        P("col"),
        P("clu", "col"),
        P("clu"),
        P("clu", None),
        P("clu", None),
        P("clu", None, None),
        P("clu", None),
        P("clu", None),
    )
    return jax.shard_map(
        functools.partial(local, n=mesh.shape["clu"], ncol=mesh.shape["col"]),
        mesh=mesh,
        in_specs=placed,
        out_specs=(P("clu", None), P("clu", "col"), P(None, "col"), P("col")),
        check_vma=False,
    )
```

profile of v0, /device:TPU:12, one launch (start us, length us, event | category | flops | bytes accessed | tf_op | source)
XLA Modules:
  0.0 152.5 jit_solution(11472327379950058459)
XLA Ops:
  0.6 1.3 broadcast_in_dim.11
  1.9 1.8 %copy.14.lidx = s32[1024,16]{1,0:T(8,128)} copy(s32[1024,16]{0,1:T(8,128)} %param.15) | data formatting | bytes 131072 | tf_op args[5]
  3.7 1.8 %copy.15.lwgt = f32[1024,16]{1,0:T(8,128)} copy(f32[1024,16]{0,1:T(8,128)} %param.16) | data formatting | bytes 131072 | tf_op args[6]
  5.6 1.8 %copy.16.ridx = s32[1024,8]{1,0:T(8,128)} copy(s32[1024,8]{0,1:T(8,128)} %param.18) | data formatting | bytes 65536 | tf_op args[8]
  7.3 1.7 %copy.17.rwgt = f32[1024,8]{1,0:T(8,128)} copy(f32[1024,8]{0,1:T(8,128)} %param.19) | data formatting | bytes 65536 | tf_op args[9]
  9.1 135.5 %shard_map.129 = (bf16[1024,2048]{1,0:T(8,128)(2,1)}, bf16[1024,512]{1,0:T(8,128)(2,1)}, bf16[8,256,512]{2,1,0:T(8,128)(2,1)}, f32[1,512]{1,0:T(1,128)}) custom-call(bf16[1024,512]{1,0:T(8,128)(2,1)} %feat.1, bf16[2048,512]{1,0:T(8,128)(2,1)} %weight_in.1, f32[1,512]{1,0:T(1,128)} %bitcast.7, bf16[1024,512]{1,0:T(8,128)(2,1)} %cot_in.1, f32[1,1024]{1,0:T(1,128)} %bitcast.9, ...), custom_call_target="tpu_custom_call" | custom-call | flops 11811160064 | bytes 16777216 | tf_op jit(solution)/shard_map/pallas_call | solution.py:484
  144.6 0.0 copy-start
  144.6 4.3 %bitcast_convert_fusion = f32[2048,512]{1,0:T(8,128)} fusion(bf16[8,256,512]{2,1,0:T(8,128)(2,1)} %get-tuple-element.10), kind=kLoop, calls=%fused_computation | loop fusion | flops 1048576 | bytes 6291456 | tf_op jit(solution)/shard_map/convert_element_type | solution.py:503
  148.9 0.0 copy-done
  148.9 0.0 copy-start.1
  148.9 0.0 copy-start.2
  149.0 2.0 %copy.21 = bf16[1024,2048]{1,0:T(8,128)(2,1)} copy(bf16[1024,2048]{1,0:T(8,128)(2,1)S(1)} %copy-done) | data formatting | bytes 8388608
  151.0 0.0 copy-done.1
  151.0 1.0 copy.22
  151.9 0.0 copy-done.2
  151.9 0.6 copy.23
Async XLA Ops:
  144.6 4.4 %copy-start = (bf16[1024,2048]{1,0:T(8,128)(2,1)S(1)}, bf16[1024,2048]{1,0:T(8,128)(2,1)}, u32[]{:S(2)}) copy-start(bf16[1024,2048]{1,0:T(8,128)(2,1)} %get-tuple-element.16) | copy-start | bytes 12582916
  148.9 2.0 %copy-start.1 = (bf16[1024,512]{1,0:T(8,128)(2,1)S(1)}, bf16[1024,512]{1,0:T(8,128)(2,1)}, u32[]{:S(2)}) copy-start(bf16[1024,512]{1,0:T(8,128)(2,1)} %get-tuple-element.17) | copy-start | bytes 3145732
  148.9 3.0 %copy-start.2 = (f32[1,512]{1,0:T(1,128)S(1)}, f32[1,512]{1,0:T(1,128)}, u32[]{:S(2)}) copy-start(f32[1,512]{1,0:T(1,128)} %get-tuple-element.11) | copy-start | bytes 6148
where the time goes:
time: 153 us
  Pallas kernels  136 us (89%)
  local copies, waits for them, and re-layouts  10.7 us (7%)
  other arithmetic  5.61 us (4%)
    pallas_call x1, Pallas kernels, local(): pl.pallas_call(functools.partial(layer, n=n, ncol=ncol), out_shape=(jax.S...  136 us
    unnamed x13, local copies, waits for them, and re-layouts  10.7 us
    convert_element_type x1, other arithmetic, local(): return (act, ig, wg.reshape(width, part).astype(f32), bg[0])  4.35 us

commit v1 on v0

--- a/solution.py
+++ b/solution.py
@@ -30,11 +30,11 @@
 
 def layer(
     feat, weight_in, bias, cot_in, selfw, lidx, lwgt, send, ridx, rwgt,
-    act_out, ig_out, wg_out, bg_out,
-    w_v, cot_v, sel, near, far, edge_pos, edge_w, outg, incg, wide, merged, act, glow, keep_own, keep_far,
-    csend, crecv, xsend, xrecv, gm, wacc, ysend, yrecv, zsend, zrecv, wfin, bsend, brecv, ret,
+    act, ig_out, wfin, bg_out,
+    w_v, cot_v, sel, near, far, edge_pos, edge_w, outg, incg, wide, merged, glow, keep_own, keep_far,
+    csend, crecv, xsend, xrecv, gm, wacc, ysend, yrecv, zsend, zrecv, bsend, brecv, ret,
     load_s, in_s, in_r, tab_s, tab_r, mx_s, mx_r, mc_s, mc_r, mf_s, mf_r, rc_s, rc_r, rx_s, rx_r,
-    y_s, y_r, z_s, z_r, zg_s, zg_r, yg_s, yg_r, b_s, b_r, ret_s, ret_r, ax_s, ax_r, ac_s, ac_r, af_s, af_r, out_s,
+    y_s, y_r, z_s, z_r, zg_s, zg_r, yg_s, yg_r, b_s, b_r, ret_s, ret_r, ax_s, ax_r, ac_s, ac_r, af_s, af_r,
     *, n, ncol,
 ):
     rows, part = feat.shape
@@ -114,7 +114,7 @@
         peers(functools.partial(in_copy, h))
         incg[h, me] = jnp.zeros((slots, half), bf16)
 
-    local_edges, far_edges = lidx.shape[1], ridx.shape[1]
+    local_edges, far_edges = lidx.shape[0], ridx.shape[0]
     first_far = local_edges + 1
 
     def put_edges(at, idx, w):
@@ -122,9 +122,9 @@
             edge_pos[at + k] = jnp.broadcast_to(idx[k : k + 1, :], (8, rows))
             edge_w[at + k] = jnp.broadcast_to(w[k : k + 1, :], (8, rows))
 
-    put_edges(0, lidx[...].T, lwgt[...].T)
+    put_edges(0, lidx[...], lwgt[...])
     put_edges(local_edges, lax.broadcasted_iota(i32, (1, rows), 1), (1.0 + enhance) * selfw[...])
-    put_edges(first_far, ridx[...].T, rwgt[...].T)
+    put_edges(first_far, ridx[...], rwgt[...])
     sub = lax.broadcasted_iota(i32, (8, 128), 0)
 
     def table(dst, first, count, base, edge_from, edge_to):
@@ -227,7 +227,7 @@
 
     def first_half(r):
         whole_rows(0, r)
-        wide[r * rb : (r + 1) * rb, :] = products(0, r) + bias[...]
+        wide[r * rb : (r + 1) * rb, :] = products(0, r) + bias[...].astype(f32)
 
     def second_half(r):
         whole_rows(1, r)
@@ -346,9 +346,6 @@
 
     own_act = act.at[col]
     put(own_act, own_act, ac_s.at[0], ac_r.at[0], (me, pair))
-    columns = lambda q: pl.ds(pl.multiple_of(q * part, part), part)
-    saves = [pltpu.make_async_copy(own_act, act_out.at[:, columns(col)], out_s.at[0])]
-    saves[0].start()
 
     for k in order[: depth - 3]:
         weight_pass(k)
@@ -422,29 +419,43 @@
         got(piece, ax_r.at[r])
         put(piece, piece, af_s.at[r], af_r.at[r], (me, pair))
     got(act.at[pair], ac_r.at[0])
-    for at, q in enumerate((pair, xcol)):
-        saves.append(pltpu.make_async_copy(act.at[q], act_out.at[:, columns(q)], out_s.at[1 + at]))
-        saves[-1].start()
     peers(lambda s: got(brecv.at[s], b_r.at[s]))
     brecv[me] = bsend[...]
     bg_out[...] = jnp.sum(brecv[...].reshape(n * 8, part), axis=0, keepdims=True)
     for r in range(BLOCKS):
         got(act.at[dcol, pl.ds(r * rb, rb)], af_r.at[r])
-    saves.append(pltpu.make_async_copy(act.at[dcol], act_out.at[:, columns(dcol)], out_s.at[3]))
-    saves[-1].start()
     for k in range(depth):
         z = place(k)
         got(wfin.at[z * 2 + 1 - yy], yg_r.at[z])
-    saves.append(pltpu.make_async_copy(wfin, wg_out, out_s.at[4]))
-    saves[-1].start()
 
     peers(lambda t: sent(bsend, b_s.at[t]))
     for h in range(HALVES):
         peers(lambda t: sent(outg.at[h, t], ret_s.at[h, t]))
     for copy in pending:
         copy.wait_send()
-    for save in saves:
-        save.wait()
+
+
+WRITES = 8
+
+
+def store(act, ig, wg, bg, act_out, ig_out, wg_out, bg_out, wide, some_s, wg_s):
+    ncol, part = act.shape[0], act.shape[2]
+    copies = []
+    for q in range(ncol):
+        copies.append(pltpu.make_async_copy(act.at[q], act_out.at[:, q * part : (q + 1) * part], some_s.at[q]))
+        copies[-1].start()
+    copies.append(pltpu.make_async_copy(ig, ig_out, some_s.at[ncol]))
+    copies[-1].start()
+    tall = wide.shape[0] // WRITES
+    group = wg.shape[0] // WRITES
+    for p in range(WRITES):
+        rs = slice(p * tall, (p + 1) * tall)
+        wide[rs, :] = wg[p * group : (p + 1) * group].reshape(tall, part).astype(f32)
+        copies.append(pltpu.make_async_copy(wide.at[rs], wg_out.at[rs], wg_s.at[p]))
+        copies[-1].start()
+    bg_out[...] = bg[...]
+    for copy in copies:
+        copy.wait()
 
 
 def local(
@@ -466,12 +477,12 @@
         V((width, part), bf16), V((rows, part), bf16), V((gs, rows), bf16), V((rows, rows), bf16), V((gs, rows), bf16),
         V((edges, 8, rows), i32), V((edges, 8, rows), f32),
         V((HALVES, n, slots, half), bf16), V((HALVES, n, slots, half), bf16), V((rows, part), f32),
-        V((ncol, HALVES, rows, half), bf16), V((ncol, rows, part), bf16), V((rows, part), bf16),
+        V((ncol, HALVES, rows, half), bf16), V((rows, part), bf16),
         V((rows, part), f32), V((rows, part), f32),
         V((BLOCKS, 2, rb, part), bf16), V((BLOCKS, 2, rb, part), bf16), V((BLOCKS, rb, part), bf16), V((BLOCKS, rb, part), bf16),
         V((rows, part), bf16), V((width, part), f32),
         V((depth, kb, part), bf16), V((depth, kb, part), bf16), V((depth, kb, part), bf16), V((depth, kb, part), bf16),
-        V((n, kb, part), bf16), V((8, part), f32), V((n, 8, part), f32), V((HALVES, n, slots, half), bf16),
+        V((8, part), f32), V((n, 8, part), f32), V((HALVES, n, slots, half), bf16),
     ]
     semaphores = [
         S(2), S(HALVES, n), S(HALVES, n), S(2), S(2),
@@ -479,28 +490,42 @@
         S(BLOCKS), S(BLOCKS), S(BLOCKS), S(BLOCKS),
         S(depth), S(depth), S(depth), S(depth), S(depth), S(depth), S(depth), S(depth),
         S(n), S(n), S(HALVES, n), S(HALVES, n),
-        S(BLOCKS), S(BLOCKS), S(1), S(1), S(BLOCKS), S(BLOCKS), S(5),
+        S(BLOCKS), S(BLOCKS), S(1), S(1), S(BLOCKS), S(BLOCKS),
     ]
-    act, ig, wg, bg = pl.pallas_call(
+    results = pl.pallas_call(
         functools.partial(layer, n=n, ncol=ncol),
+        out_shape=(
+            V((ncol, rows, part), bf16),
+            V((rows, part), bf16),
+            V((n, kb, part), bf16),
+            V((1, part), f32),
+        ),
+        in_specs=[vmem, hbm, vmem, hbm, vmem, vmem, vmem, vmem, vmem, vmem],
+        out_specs=(vmem,) * 4,
+        scratch_shapes=buffers + semaphores,
+        compiler_params=pltpu.CompilerParams(
+            collective_id=0, has_side_effects=True, vmem_limit_bytes=50 << 20
+        ),
+        cost_estimate=pl.CostEstimate(flops=11 << 30, bytes_accessed=16 << 20, transcendentals=1 << 20),
+    )(
+        features, weight, layer_bias[None, :], cotangent, self_weight[None, :], local_index.T, local_weight.T,
+        send_index[0], remote_slot.T, remote_weight.T,
+    )
+    output, input_grad, weight_grad, bias_grad = pl.pallas_call(
+        store,
         out_shape=(
             jax.ShapeDtypeStruct((rows, ncol * part), bf16),
             jax.ShapeDtypeStruct((rows, part), bf16),
-            jax.ShapeDtypeStruct((n, kb, part), bf16),
+            jax.ShapeDtypeStruct((width, part), f32),
             jax.ShapeDtypeStruct((1, part), f32),
         ),
-        in_specs=[vmem, hbm, vmem, hbm, vmem, vmem, vmem, vmem, vmem, vmem],
-        out_specs=(hbm, vmem, hbm, vmem),
-        scratch_shapes=buffers + semaphores,
-        compiler_params=pltpu.CompilerParams(
-            collective_id=0, has_side_effects=True, vmem_limit_bytes=62 << 20
-        ),
-        cost_estimate=pl.CostEstimate(flops=11 << 30, bytes_accessed=16 << 20, transcendentals=1 << 20),
-    )(
-        features, weight, layer_bias.astype(f32)[None, :], cotangent, self_weight[None, :], local_index, local_weight,
-        send_index[0], remote_slot, remote_weight,
-    )
-    return act, ig, wg.reshape(width, part).astype(f32), bg[0]
+        in_specs=[vmem] * 4,
+        out_specs=(hbm, hbm, hbm, vmem),
+        scratch_shapes=[V((width, part), f32), S(ncol + 1), S(WRITES)],
+        compiler_params=pltpu.CompilerParams(vmem_limit_bytes=6 << 20),
+        cost_estimate=pl.CostEstimate(flops=0, bytes_accessed=10 << 20, transcendentals=0),
+    )(*results)
+    return output, input_grad, weight_grad, bias_grad[0]
 
 
 def solution(mesh):

time: 153 us -> 139 us (0.908)
  local copies, waits for them, and re-layouts: 10.7 us -> 1.26 us
  other arithmetic: 5.61 us -> 0 us
    unnamed x13 -> x0, local copies, waits for them, and re-layouts: 10.7 us -> none
    convert_element_type x1 -> x0, other arithmetic: 4.35 us -> none  [local(): return (act, ig, wg.reshape(width, part).astype(f32), bg[0])]
    pallas_call x1 -> x2, Pallas kernels: 136 us -> 137 us  [the longest x1 132 us: local(): pl.pallas_call(functools.partial(layer, n=n, ncol=ncol), out_shape=(V((nc...]
where the time goes in v1:
time: 139 us; the launch traced here: 138 us
  Pallas kernels  137 us (99%)
    pallas_call x1, Pallas kernels, local(): pl.pallas_call(functools.partial(layer, n=n, ncol=ncol), out_shape=(V((nc...  132 us
    pallas_call x1, Pallas kernels, local(): pl.pallas_call(store, out_shape=(jax.ShapeDtypeStruct((rows, ncol * part)...  4.32 us

profile of v1, /device:TPU:12, one launch (start us, length us, event | category | flops | bytes accessed | tf_op | source)
XLA Modules:
  0.0 138.5 jit_solution(17324733322275977947)
XLA Ops:
  0.6 1.3 broadcast_in_dim.6.bias
  1.9 132.3 %shard_map.129 = (bf16[4,1024,512]{2,1,0:T(8,128)(2,1)S(1)}, bf16[1024,512]{1,0:T(8,128)(2,1)S(1)}, bf16[8,256,512]{2,1,0:T(8,128)(2,1)S(1)}, f32[1,512]{1,0:T(1,128)S(1)}) custom-call(bf16[1024,512]{1,0:T(8,128)(2,1)} %feat.1, bf16[2048,512]{1,0:T(8,128)(2,1)} %weight_in.1, bf16[1,512]{1,0:T(2,128)(2,1)} %broadcast_in_dim.6.bias, bf16[1024,512]{1,0:T(8,128)(2,1)} %cot_in.1, ...), custom_call_target="tpu_custom_call" | custom-call | flops 11811160064 | bytes 16777216 | tf_op jit(solution)/shard_map/pallas_call | solution.py:495
  134.2 4.3 %shard_map.130 = (bf16[1024,2048]{1,0:T(8,128)(2,1)}, bf16[1024,512]{1,0:T(8,128)(2,1)}, f32[2048,512]{1,0:T(8,128)}, f32[1,512]{1,0:T(1,128)}) custom-call(bf16[4,1024,512]{2,1,0:T(8,128)(2,1)S(1)} %get-tuple-element.12.act, bf16[1024,512]{1,0:T(8,128)(2,1)S(1)} %get-tuple-element.13.ig, bf16[8,256,512]{2,1,0:T(8,128)(2,1)S(1)} %get-tuple-element.14.wg, ...), custom_call_target="tpu_custom_call" | custom-call | bytes 10485760 | tf_op jit(solution)/shard_map/pallas_call | solution.py:514

commit v2 on v1

--- a/solution.py
+++ b/solution.py
@@ -32,9 +32,9 @@
     feat, weight_in, bias, cot_in, selfw, lidx, lwgt, send, ridx, rwgt,
     act, ig_out, wfin, bg_out,
     w_v, cot_v, sel, near, far, edge_pos, edge_w, outg, incg, wide, merged, glow, keep_own, keep_far,
-    csend, crecv, xsend, xrecv, gm, wacc, ysend, yrecv, zsend, zrecv, bsend, brecv, ret,
+    csend, crecv, xsend, xrecv, gm, wacc, ysend, yrecv, zsend, from_before, from_after, bsend, brecv, ret,
     load_s, in_s, in_r, tab_s, tab_r, mx_s, mx_r, mc_s, mc_r, mf_s, mf_r, rc_s, rc_r, rx_s, rx_r,
-    y_s, y_r, z_s, z_r, zg_s, zg_r, yg_s, yg_r, b_s, b_r, ret_s, ret_r, ax_s, ax_r, ac_s, ac_r, af_s, af_r,
+    y_s, y_r, z_s, fb_r, fa_r, zu_s, zd_s, zg_r, yg_s, yg_r, b_s, b_r, ret_s, ret_r, ax_s, ax_r, ac_s, ac_r, af_s, af_r,
     *, n, ncol,
 ):
     rows, part = feat.shape
@@ -57,12 +57,15 @@
     ypeer = (me + 1 - 2 * yy, col)
     pending = []
 
-    def put(src, dst, ss, rs, dev):
+    def start(src, dst, ss, rs, dev):
         copy = pltpu.make_async_remote_copy(
             src_ref=src, dst_ref=dst, send_sem=ss, recv_sem=rs, device_id=dev, device_id_type=MESH
         )
         copy.start()
-        pending.append(copy)
+        return copy
+
+    def put(*args):
+        pending.append(start(*args))
 
     def got(dst, rs):
         pltpu.make_async_remote_copy(
@@ -290,9 +293,11 @@
 
     bsend[...] = total
 
-    def weight_chunk(chunk):
-        q, h = lax.div(chunk, HALVES), lax.rem(chunk, HALVES)
-        return tn(merged[q, h], glow[...])
+    def cols(h):
+        return slice(h * half, (h + 1) * half)
+
+    def weight_chunk(chunk, h):
+        return tn(merged[lax.div(chunk, HALVES), lax.rem(chunk, HALVES)], glow[:, cols(h)])
 
     fine = kb == half
     if not fine:
@@ -302,35 +307,112 @@
     def block_rows(b):
         return pl.ds(pl.multiple_of(b * kb, kb), kb)
 
+    low = zz < depth // 2
+    ahead = jnp.where(low, depth - 1 - zz, zz)
+
     def place(k):
-        return lax.rem(zz + k, depth)
-
-    def weight_out(k):
+        up = jnp.where(k < ahead, depth - 1 - k, k - ahead)
+        return jnp.where(low, up, depth - 1 - up)
+
+    def weight_out(h, k):
         z = place(k)
         theirs, mine = z * 2 + 1 - yy, z * 2 + yy
         if fine:
-            ysend[z] = weight_chunk(theirs).astype(bf16)
+            ysend[h, z] = weight_chunk(theirs, h).astype(bf16)
         else:
-            ysend[z] = wacc[block_rows(theirs), :].astype(bf16)
-        put(ysend.at[z], yrecv.at[z], y_s.at[z], y_r.at[z], ypeer)
+            ysend[h, z] = wacc[block_rows(theirs), cols(h)].astype(bf16)
+        put(ysend.at[h, z], yrecv.at[h, z], y_s.at[h, z], y_r.at[h, z], ypeer)
         if fine:
-            wacc[block_rows(mine), :] = weight_chunk(mine)
-
-    def weight_pass(k):
+            wacc[block_rows(mine), cols(h)] = weight_chunk(mine, h)
+
+    before, after = me - 2, me + 2
+
+    def weight_sum(h, k):
         z = place(k)
-        got(yrecv.at[z], y_r.at[z])
-        summed = wacc[block_rows(z * 2 + yy), :] + yrecv[z].astype(f32)
-        if k:
-            zsend[z] = summed.astype(bf16)
-            put(zsend.at[z], zrecv.at[zz], z_s.at[z], z_r.at[zz], (z * 2 + yy, col))
-        else:
-            wacc[block_rows(me), :] = summed
-
-    order = list(range(1, depth)) + [0]
-    for at, k in enumerate(order):
-        weight_out(k)
-        if at == 0:
-            grads_over(BLOCKS - 1)
+        got(yrecv.at[h, z], y_r.at[h, z])
+        total = wacc[block_rows(z * 2 + yy), cols(h)] + yrecv[h, z].astype(f32)
+        if k == depth - 1:
+            wacc[block_rows(me), cols(h)] = total
+
+            @pl.when(zz > 0)
+            def _():
+                got(from_before.at[h, zz], fb_r.at[h, zz])
+                wacc[block_rows(me), cols(h)] += from_before[h, zz].astype(f32)
+
+            @pl.when(zz < depth - 1)
+            def _():
+                got(from_after.at[h, zz], fa_r.at[h, zz])
+                wacc[block_rows(me), cols(h)] += from_after[h, zz].astype(f32)
+
+            wfin[h, me] = wacc[block_rows(me), cols(h)].astype(bf16)
+            weight_share(h, me)
+            return
+        zsend[h, z] = total.astype(bf16)
+
+        @pl.when(z > zz)
+        def _():
+            @pl.when(zz > 0)
+            def _():
+                got(from_before.at[h, z], fb_r.at[h, z])
+                zsend[h, z] = (total + from_before[h, z].astype(f32)).astype(bf16)
+
+            start(zsend.at[h, z], from_before.at[h, z], z_s.at[h, z], fb_r.at[h, z], (after, col))
+
+        @pl.when(z < zz)
+        def _():
+            @pl.when(zz < depth - 1)
+            def _():
+                got(from_after.at[h, z], fa_r.at[h, z])
+                zsend[h, z] = (total + from_after[h, z].astype(f32)).astype(bf16)
+
+            start(zsend.at[h, z], from_after.at[h, z], z_s.at[h, z], fa_r.at[h, z], (before, col))
+
+    def weight_share(h, b, up=True, down=True):
+        z = lax.div(b, 2)
+        block = wfin.at[h, b]
+        if up:
+            @pl.when(zz < depth - 1)
+            def _():
+                start(block, block, zu_s.at[h, z], zg_r.at[h, z], (after, col))
+        if down:
+            @pl.when(zz > 0)
+            def _():
+                start(block, block, zd_s.at[h, z], zg_r.at[h, z], (before, col))
+        start(block, block, yg_s.at[h, z], yg_r.at[h, z], ypeer)
+
+    def weight_on(h, d):
+        @pl.when(zz >= d)
+        def _():
+            got(wfin.at[h, me - 2 * d], zg_r.at[h, zz - d])
+            weight_share(h, me - 2 * d, down=False)
+
+        @pl.when(zz + d < depth)
+        def _():
+            got(wfin.at[h, me + 2 * d], zg_r.at[h, zz + d])
+            weight_share(h, me + 2 * d, up=False)
+
+    def weight_end(h):
+        for z in range(depth):
+            got(wfin.at[h, z * 2 + 1 - yy], yg_r.at[h, z])
+            sent(wfin.at[h, z * 2 + yy], yg_s.at[h, z])
+
+            @pl.when(z != zz)
+            def _():
+                sent(zsend.at[h, z], z_s.at[h, z])
+
+            @pl.when((z <= zz) & (zz < depth - 1))
+            def _():
+                sent(wfin.at[h, z * 2 + yy], zu_s.at[h, z])
+
+            @pl.when((z >= zz) & (zz > 0))
+            def _():
+                sent(wfin.at[h, z * 2 + yy], zd_s.at[h, z])
+
+    for h in range(HALVES):
+        for k in range(depth):
+            weight_out(h, k)
+            if h == 0 and k == 0:
+                grads_over(BLOCKS - 1)
 
     def bias_copy(t):
         pltpu.make_async_remote_copy(
@@ -347,14 +429,16 @@
     own_act = act.at[col]
     put(own_act, own_act, ac_s.at[0], ac_r.at[0], (me, pair))
 
-    for k in order[: depth - 3]:
-        weight_pass(k)
+    steps = [functools.partial(weight_sum, h, k) for h in range(HALVES) for k in range(depth)]
+    steps.pop(0)()
     grads_in(0)
+    steps.pop(0)()
     grads_in(1)
-    weight_pass(order[depth - 3])
+    for _ in range(depth - 2):
+        steps.pop(0)()
     grads_in(2)
     act_over(0)
-    weight_pass(order[depth - 2])
+    steps.pop(0)()
     grads_in(3)
     for r in range(1, BLOCKS):
         act_over(r)
@@ -380,22 +464,15 @@
     for h in range(HALVES):
         peers(functools.partial(back_copy, h))
         ret[h, me] = jnp.zeros((slots, half), bf16)
-    weight_pass(0)
+    for k in range(1, depth - 1):
+        steps.pop(0)()
+        weight_on(0, k)
     for r in range(BLOCKS):
         rs = slice(r * rb, (r + 1) * rb)
         wide[rs, :] = nn(near[rs, :], gm[...])
-
-    mine = wacc[block_rows(me), :]
-    for k in range(1, depth):
-        z = place(k)
-        got(zrecv.at[z], z_r.at[z])
-        mine = mine + zrecv[z].astype(f32)
-    wfin[me] = mine.astype(bf16)
-    block = wfin.at[me]
-    for k in range(1, depth):
-        z = place(k)
-        put(block, block, zg_s.at[z], zg_r.at[zz], (z * 2 + yy, col))
-    put(block, block, yg_s.at[zz], yg_r.at[zz], ypeer)
+    steps.pop(0)()
+    weight_on(0, depth - 1)
+    weight_on(1, 1)
 
     for h in range(HALVES):
         hs = slice(h * half, (h + 1) * half)
@@ -409,11 +486,8 @@
                 wide[rs, hs] += tn(sel[:, rs], back)
         ig_out[:, hs] = wide[:, hs].astype(bf16)
 
-    for k in range(1, depth):
-        z = place(k)
-        block = wfin.at[z * 2 + yy]
-        got(block, zg_r.at[z])
-        put(block, block, yg_s.at[z], yg_r.at[z], ypeer)
+    for d in range(2, depth):
+        weight_on(1, d)
     for r in range(BLOCKS):
         piece = act.at[xcol, pl.ds(r * rb, rb)]
         got(piece, ax_r.at[r])
@@ -424,9 +498,8 @@
     bg_out[...] = jnp.sum(brecv[...].reshape(n * 8, part), axis=0, keepdims=True)
     for r in range(BLOCKS):
         got(act.at[dcol, pl.ds(r * rb, rb)], af_r.at[r])
-    for k in range(depth):
-        z = place(k)
-        got(wfin.at[z * 2 + 1 - yy], yg_r.at[z])
+    for h in range(HALVES):
+        weight_end(h)
 
     peers(lambda t: sent(bsend, b_s.at[t]))
     for h in range(HALVES):
@@ -447,10 +520,11 @@
     copies.append(pltpu.make_async_copy(ig, ig_out, some_s.at[ncol]))
     copies[-1].start()
     tall = wide.shape[0] // WRITES
-    group = wg.shape[0] // WRITES
+    group, half = wg.shape[1] // WRITES, wg.shape[3]
     for p in range(WRITES):
         rs = slice(p * tall, (p + 1) * tall)
-        wide[rs, :] = wg[p * group : (p + 1) * group].reshape(tall, part).astype(f32)
+        for h in range(HALVES):
+            wide[rs, h * half : (h + 1) * half] = wg[h, p * group : (p + 1) * group].reshape(tall, half).astype(f32)
         copies.append(pltpu.make_async_copy(wide.at[rs], wg_out.at[rs], wg_s.at[p]))
         copies[-1].start()
     bg_out[...] = bg[...]
@@ -481,14 +555,14 @@
         V((rows, part), f32), V((rows, part), f32),
         V((BLOCKS, 2, rb, part), bf16), V((BLOCKS, 2, rb, part), bf16), V((BLOCKS, rb, part), bf16), V((BLOCKS, rb, part), bf16),
         V((rows, part), bf16), V((width, part), f32),
-        V((depth, kb, part), bf16), V((depth, kb, part), bf16), V((depth, kb, part), bf16), V((depth, kb, part), bf16),
+        *[V((HALVES, depth, kb, half), bf16) for _ in range(5)],
         V((8, part), f32), V((n, 8, part), f32), V((HALVES, n, slots, half), bf16),
     ]
     semaphores = [
         S(2), S(HALVES, n), S(HALVES, n), S(2), S(2),
         S(HALVES, BLOCKS), S(HALVES, BLOCKS), S(HALVES, BLOCKS), S(HALVES, BLOCKS), S(HALVES, BLOCKS), S(HALVES, BLOCKS),
         S(BLOCKS), S(BLOCKS), S(BLOCKS), S(BLOCKS),
-        S(depth), S(depth), S(depth), S(depth), S(depth), S(depth), S(depth), S(depth),
+        *[S(HALVES, depth) for _ in range(10)],
         S(n), S(n), S(HALVES, n), S(HALVES, n),
         S(BLOCKS), S(BLOCKS), S(1), S(1), S(BLOCKS), S(BLOCKS),
     ]
@@ -497,14 +571,14 @@
         out_shape=(
             V((ncol, rows, part), bf16),
             V((rows, part), bf16),
-            V((n, kb, part), bf16),
+            V((HALVES, n, kb, half), bf16),
             V((1, part), f32),
         ),
         in_specs=[vmem, hbm, vmem, hbm, vmem, vmem, vmem, vmem, vmem, vmem],
         out_specs=(vmem,) * 4,
         scratch_shapes=buffers + semaphores,
         compiler_params=pltpu.CompilerParams(
-            collective_id=0, has_side_effects=True, vmem_limit_bytes=50 << 20
+            collective_id=0, has_side_effects=True, vmem_limit_bytes=54 << 20
         ),
         cost_estimate=pl.CostEstimate(flops=11 << 30, bytes_accessed=16 << 20, transcendentals=1 << 20),
     )(

time: 139 us -> 122 us (0.88)
  the two profiles are of different devices: /device:TPU:12 before, /device:TPU:0 now
where the time goes in v2:
time: 122 us
  Pallas kernels  120 us (98%)
  local copies, waits for them, and re-layouts  1.26 us (1%)
    pallas_call x1, Pallas kernels, local(): pl.pallas_call(functools.partial(layer, n=n, ncol=ncol), out_shape=(V((nc...  115 us
    pallas_call x1, Pallas kernels, local(): pl.pallas_call(store, out_shape=(jax.ShapeDtypeStruct((rows, ncol * part)...  4.32 us

profile of v2, /device:TPU:0, one launch (start us, length us, event | category | flops | bytes accessed | tf_op | source)
XLA Modules:
  0.0 121.8 jit_solution(18283115567210867401)
XLA Ops:
  0.6 1.3 %broadcast_in_dim.6.bias = bf16[1,512]{1,0:T(2,128)(2,1)} reshape(bf16[512]{0:T(512)(128)(2,1)} %param.12) | data formatting | bytes 2048 | tf_op jit(solution)/shard_map/broadcast_in_dim | solution.py:585
  1.9 115.4 %shard_map.129 = (bf16[4,1024,512]{2,1,0:T(8,128)(2,1)S(1)}, bf16[1024,512]{1,0:T(8,128)(2,1)S(1)}, bf16[2,8,256,256]{3,2,1,0:T(8,128)(2,1)S(1)}, f32[1,512]{1,0:T(1,128)S(1)}) custom-call(bf16[1024,512]{1,0:T(8,128)(2,1)} %feat.1, bf16[2048,512]{1,0:T(8,128)(2,1)} %weight_in.1, bf16[1,512]{1,0:T(2,128)(2,1)} %broadcast_in_dim.6.bias, ...), custom_call_target="tpu_custom_call" | custom-call | flops 11811160064 | bytes 16777216 | tf_op jit(solution)/shard_map/pallas_call | solution.py:569
  117.3 4.3 %shard_map.130 = (bf16[1024,2048]{1,0:T(8,128)(2,1)}, bf16[1024,512]{1,0:T(8,128)(2,1)}, f32[2048,512]{1,0:T(8,128)}, f32[1,512]{1,0:T(1,128)}) custom-call(bf16[4,1024,512]{2,1,0:T(8,128)(2,1)S(1)} %get-tuple-element.12.act, bf16[1024,512]{1,0:T(8,128)(2,1)S(1)} %get-tuple-element.13.ig, bf16[2,8,256,256]{3,2,1,0:T(8,128)(2,1)S(1)} %get-tuple-element.14.wg, ...), custom_call_target="tpu_custom_call" | custom-call | bytes 10485760 | tf_op jit(solution)/shard_map/pallas_call | solution.py:588

commit v3 on v2

--- a/solution.py
+++ b/solution.py
@@ -13,7 +13,12 @@
 MESH = pl.DeviceIdType.MESH
 BLOCKS = 4
 HALVES = 2
+QUARTERS = 4
 UNROLL = 8
+ORDER = (
+    (0, 0), (0, 1), (1, 0), (1, 1), (0, 2), (1, 2), (2, 0), (2, 1), (2, 2),
+    (3, 0), (0, 3), (3, 1), (1, 3), (3, 2), (2, 3), (3, 3),
+)
 
 
 def tn(a, b):
@@ -31,14 +36,15 @@
 def layer(
     feat, weight_in, bias, cot_in, selfw, lidx, lwgt, send, ridx, rwgt,
     act, ig_out, wfin, bg_out,
-    w_v, cot_v, sel, near, far, edge_pos, edge_w, outg, incg, wide, merged, glow, keep_own, keep_far,
+    w_v, cot_v, sel, near, far, turned, edge_pos, edge_w, outg, incg, wide, merged, glow, keep_own, keep_far,
     csend, crecv, xsend, xrecv, gm, wacc, ysend, yrecv, zsend, from_before, from_after, bsend, brecv, ret,
     load_s, in_s, in_r, tab_s, tab_r, mx_s, mx_r, mc_s, mc_r, mf_s, mf_r, rc_s, rc_r, rx_s, rx_r,
     y_s, y_r, z_s, fb_r, fa_r, zu_s, zd_s, zg_r, yg_s, yg_r, b_s, b_r, ret_s, ret_r, ax_s, ax_r, ac_s, ac_r, af_s, af_r,
     *, n, ncol,
 ):
     rows, part = feat.shape
-    half = part // HALVES
+    half, quarter = part // HALVES, part // QUARTERS
+    per_half = QUARTERS // HALVES
     rb = rows // BLOCKS
     slots = send.shape[1]
     gd = min(8, n)
@@ -100,22 +106,29 @@
         for d in range(gd):
             sel[d * slots : (d + 1) * slots, :] = jnp.where(ids[:, d : d + 1] == lane, 1.0, 0.0).astype(bf16)
 
-    def in_copy(h, t):
+    def half_of(ref, h, *at):
+        return jnp.concatenate([ref[(h * per_half + p, *at)] for p in range(per_half)], axis=-1)
+
+    def in_copy(q, t):
         pltpu.make_async_remote_copy(
-            src_ref=outg.at[h, t], dst_ref=incg.at[h, me], send_sem=in_s.at[h, t], recv_sem=in_r.at[h, me],
+            src_ref=outg.at[q, t], dst_ref=incg.at[q, me], send_sem=in_s.at[q, t], recv_sem=in_r.at[q, me],
             device_id=(t, col), device_id_type=MESH,
         ).start()
 
-    for h in range(HALVES):
-        for g in range(groups):
-            if groups > 1 or h == 0:
-                put_selector(g)
-            rows_out = nn(sel[...], feat[:, h * half : (h + 1) * half]).astype(bf16)
-            outg[h, g * gd : (g + 1) * gd] = rows_out.reshape(gd, slots, half)
-        if h == 0:
+    for q in range(QUARTERS):
+        if q % per_half == 0:
+            for g in range(groups):
+                if groups > 1 or q == 0:
+                    put_selector(g)
+                at = q // per_half * half
+                rows_out = nn(sel[...], feat[:, at : at + half]).astype(bf16)
+                for p in range(per_half):
+                    piece = rows_out[:, p * quarter : (p + 1) * quarter].reshape(gd, slots, quarter)
+                    outg[q // per_half * per_half + p, g * gd : (g + 1) * gd] = piece
+        if q == 0:
             pl.semaphore_wait(barrier, n + 1)
-        peers(functools.partial(in_copy, h))
-        incg[h, me] = jnp.zeros((slots, half), bf16)
+        peers(functools.partial(in_copy, q))
+        incg[q, me] = jnp.zeros((slots, quarter), bf16)
 
     local_edges, far_edges = lidx.shape[0], ridx.shape[0]
     first_far = local_edges + 1
@@ -130,7 +143,7 @@
     put_edges(first_far, ridx[...], rwgt[...])
     sub = lax.broadcasted_iota(i32, (8, 128), 0)
 
-    def table(dst, first, count, base, edge_from, edge_to):
+    def table(dst, block, first, count, base, edge_from, edge_to):
         tall = 16 * UNROLL
 
         def lanes(l, carry):
@@ -143,94 +156,125 @@
                 for k in range(edge_from, edge_to):
                     at, w = edge_pos[k, :, ls], edge_w[k, :, ls]
                     sums = [s + jnp.where(at == p, w, 0.0) for s, p in zip(sums, places)]
-                dst[pl.ds(pl.multiple_of(r0, 16), tall), ls] = jnp.concatenate(sums, 0).astype(bf16)
+                inner = pl.ds(pl.multiple_of(l * 128 - block * rb, 128), 128)
+                dst[block, pl.ds(pl.multiple_of(r0, 16), tall), inner] = jnp.concatenate(sums, 0).astype(bf16)
                 return carry
 
             return lax.fori_loop(0, count // tall, step, carry)
 
-        lax.fori_loop(0, rows // 128, lanes, 0)
-
-    def shared_table(dst, which, edge_from, edge_to):
-        count = dst.shape[0] // 2
-        table(dst, core * count, count, 0, edge_from, edge_to)
-        mine = dst.at[pl.ds(pl.multiple_of(core * count, count), count)]
-        put(mine, mine, tab_s.at[which], tab_r.at[which], (me, pair))
-
-    def wait_table(dst, which):
-        count = dst.shape[0] // 2
-        got(dst.at[pl.ds(pl.multiple_of((1 - core) * count, count), count)], tab_r.at[which])
+        lax.fori_loop(block * rb // 128, (block + 1) * rb // 128, lanes, 0)
+
+    def shared_part(dst, r, whose):
+        count = dst.shape[1] // 2
+        return dst.at[r, pl.ds(pl.multiple_of(whose * count, count), count)]
+
+    def shared_table(dst, which, r, edge_from, edge_to):
+        count = dst.shape[1] // 2
+        table(dst, r, core * count, count, 0, edge_from, edge_to)
+        piece = shared_part(dst, r, core)
+        put(piece, piece, tab_s.at[which, r], tab_r.at[which, r], (me, pair))
 
     def far_group(g):
-        table(far, 0, gs, g * gs, first_far, first_far + far_edges)
-
-    shared_table(near, 0, 0, first_far)
-    if groups == 1:
-        shared_table(far, 1, first_far, first_far + far_edges)
-    wait_table(near, 0)
-    for r in range(BLOCKS):
+        for r in range(BLOCKS):
+            table(far, r, 0, gs, g * gs, first_far, first_far + far_edges)
+
+    def build(r):
+        shared_table(near, 0, r, 0, first_far)
+        if groups == 1:
+            shared_table(far, 1, r, first_far, first_far + far_edges)
+
+    def ready(r):
         rs = slice(r * rb, (r + 1) * rb)
-        wide[rs, :] = tn(near[:, rs], feat[...])
-    if groups == 1:
-        wait_table(far, 1)
-
-    def arrived(h):
-        peers(lambda s: got(incg.at[h, s], in_r.at[h, s]))
-
-    def send_merged(h, r):
-        piece = merged.at[col, h, pl.ds(r * rb, rb)]
-        put(piece, piece, mx_s.at[h, r], mx_r.at[h, r], (me, xcol))
-        put(piece, piece, mc_s.at[h, r], mc_r.at[h, r], (me, pair))
-
-    if groups == 1:
-        for h in range(HALVES):
-            hs = slice(h * half, (h + 1) * half)
-            arrived(h)
-            pooled = incg[h].reshape(gs, half)
+        got(shared_part(near, r, 1 - core), tab_r.at[0, r])
+        wide[rs, :] = tn(near[r], feat[...])
+        if groups == 1:
+            got(shared_part(far, r, 1 - core), tab_r.at[1, r])
+            turned[rs, :] = far[r].T
+
+    def arrived(q):
+        peers(lambda s: got(incg.at[q, s], in_r.at[q, s]))
+
+    def piece_of(owner, q, r):
+        return merged.at[owner, q, pl.ds(r * rb, rb)]
+
+    def aggregate(q, r):
+        rs = slice(r * rb, (r + 1) * rb)
+        total = wide[rs, q * quarter : (q + 1) * quarter]
+        if groups == 1:
+            total = total + nn(turned[rs, :], incg[q].reshape(gs, quarter))
+        merged[col, q, rs] = total.astype(bf16)
+        piece = piece_of(col, q, r)
+        put(piece, piece, mx_s.at[q, r], mx_r.at[q, r], (me, xcol))
+        put(piece, piece, mc_s.at[q, r], mc_r.at[q, r], (me, pair))
+
+    build(0)
+    build(1)
+    ready(0)
+    if groups > 1:
+        for r in range(2, BLOCKS):
+            build(r)
+        for r in range(1, BLOCKS):
+            ready(r)
+        for q in range(QUARTERS):
+            arrived(q)
+        for g in range(groups):
+            far_group(g)
             for r in range(BLOCKS):
                 rs = slice(r * rb, (r + 1) * rb)
-                merged[col, h, rs] = (wide[rs, hs] + tn(far[:, rs], pooled)).astype(bf16)
-                send_merged(h, r)
+                turned[...] = far[r].T
+                for q in range(QUARTERS):
+                    pooled = incg[q, g * gd : (g + 1) * gd].reshape(gs, quarter)
+                    wide[rs, q * quarter : (q + 1) * quarter] += nn(turned[...], pooled)
+        for q, r in ORDER:
+            aggregate(q, r)
     else:
-        for h in range(HALVES):
-            arrived(h)
-        for g in range(groups):
-            far_group(g)
-            for h in range(HALVES):
-                hs = slice(h * half, (h + 1) * half)
-                pooled = incg[h, g * gd : (g + 1) * gd].reshape(gs, half)
-                for r in range(BLOCKS):
-                    rs = slice(r * rb, (r + 1) * rb)
-                    wide[rs, hs] += tn(far[:, rs], pooled)
-        for h in range(HALVES):
-            hs = slice(h * half, (h + 1) * half)
-            for r in range(BLOCKS):
-                rs = slice(r * rb, (r + 1) * rb)
-                merged[col, h, rs] = wide[rs, hs].astype(bf16)
-                send_merged(h, r)
+        arrived(0)
+        aggregate(0, 0)
+        ready(1)
+        aggregate(0, 1)
+        build(2)
+        arrived(1)
+        aggregate(1, 0)
+        aggregate(1, 1)
+        ready(2)
+        aggregate(0, 2)
+        aggregate(1, 2)
+        build(3)
+        arrived(2)
+        for r in range(3):
+            aggregate(2, r)
+        ready(3)
+        arrived(3)
+        for q, r in ORDER[9:]:
+            aggregate(q, r)
 
     load_w.wait()
     load_c.wait()
 
-    def cross(h, r):
-        piece = merged.at[xcol, h, pl.ds(r * rb, rb)]
-        got(piece, mx_r.at[h, r])
-        put(piece, piece, mf_s.at[h, r], mf_r.at[h, r], (me, pair))
+    def cross(count):
+        for q, r in [crossing.pop(0) for _ in range(count)]:
+            piece = piece_of(xcol, q, r)
+            got(piece, mx_r.at[q, r])
+            put(piece, piece, mf_s.at[q, r], mf_r.at[q, r], (me, pair))
 
     def whole_rows(h, r):
-        got(merged.at[pair, h, pl.ds(r * rb, rb)], mc_r.at[h, r])
-        got(merged.at[dcol, h, pl.ds(r * rb, rb)], mf_r.at[h, r])
+        for q in range(h * per_half, (h + 1) * per_half):
+            got(piece_of(pair, q, r), mc_r.at[q, r])
+            got(piece_of(dcol, q, r), mf_r.at[q, r])
+
+    crossing = list(ORDER)
 
     def products(h, r):
         total = None
         for q in range(ncol):
             k0 = q * part + h * half
-            term = nn(merged[q, h, r * rb : (r + 1) * rb, :], w_v[k0 : k0 + half, :])
+            term = nn(half_of(merged.at[q], h, slice(r * rb, (r + 1) * rb)), w_v[k0 : k0 + half, :])
             total = term if total is None else total + term
         return total
 
     def first_half(r):
         whole_rows(0, r)
-        wide[r * rb : (r + 1) * rb, :] = products(0, r) + bias[...].astype(f32)
+        wide[r * rb : (r + 1) * rb, :] = products(0, r) + bias[...].astype(f32).reshape(1, part)
 
     def second_half(r):
         whole_rows(1, r)
@@ -276,33 +320,43 @@
         got(xrecv.at[r], rx_r.at[r])
         gm[rs, :] = (keep_own[rs, :] + xrecv[r].astype(f32)).astype(bf16)
 
-    for r in range(BLOCKS):
-        cross(0, r)
-        if r:
-            first_half(r - 1)
     total = jnp.zeros((8, part), f32)
-    for r in range(BLOCKS):
-        cross(1, r)
-        if r == 0:
-            first_half(BLOCKS - 1)
-        else:
-            grads_over(r - 1)
-        second_half(r)
-        total = smooth(r, total)
-        grads(r)
-
-    bsend[...] = total
+    cross(4)
+    first_half(0)
+    cross(2)
+    first_half(1)
+    cross(3)
+    first_half(2)
+    cross(2)
+    second_half(0)
+    total = smooth(0, total)
+    cross(2)
+    second_half(1)
+    total = smooth(1, total)
+    first_half(3)
+    cross(2)
+    second_half(2)
+    total = smooth(2, total)
+    grads(0)
+    cross(1)
+    second_half(3)
+    total = smooth(3, total)
+
+    bsend[...] = jnp.sum(total, axis=0, keepdims=True)
 
     def cols(h):
         return slice(h * half, (h + 1) * half)
 
     def weight_chunk(chunk, h):
-        return tn(merged[lax.div(chunk, HALVES), lax.rem(chunk, HALVES)], glow[:, cols(h)])
+        q, at = lax.div(chunk, HALVES), lax.rem(chunk, HALVES) * per_half
+        rows_in = jnp.concatenate([merged[q, at + p] for p in range(per_half)], axis=1)
+        return tn(rows_in, glow[:, cols(h)])
 
     fine = kb == half
     if not fine:
         for chunk in range(ncol * HALVES):
-            wacc[chunk * half : (chunk + 1) * half, :] = tn(merged[chunk // HALVES, chunk % HALVES], glow[...])
+            rows_in = half_of(merged.at[chunk // HALVES], chunk % HALVES)
+            wacc[chunk * half : (chunk + 1) * half, :] = tn(rows_in, glow[...])
 
     def block_rows(b):
         return pl.ds(pl.multiple_of(b * kb, kb), kb)
@@ -408,11 +462,15 @@
             def _():
                 sent(wfin.at[h, z * 2 + yy], zd_s.at[h, z])
 
-    for h in range(HALVES):
-        for k in range(depth):
-            weight_out(h, k)
-            if h == 0 and k == 0:
-                grads_over(BLOCKS - 1)
+    rest = [functools.partial(weight_out, h, k) for h in range(HALVES) for k in range(depth)]
+    for r in range(1, BLOCKS):
+        rest.pop(0)()
+        grads_over(r - 1)
+        grads(r)
+    rest.pop(0)()
+    grads_over(BLOCKS - 1)
+    for step in rest:
+        step()
 
     def bias_copy(t):
         pltpu.make_async_remote_copy(
@@ -443,51 +501,53 @@
     for r in range(1, BLOCKS):
         act_over(r)
 
-    def sent_in(h):
-        peers(lambda t: sent(outg.at[h, t], in_s.at[h, t]))
-
-    for h in range(HALVES):
-        sent_in(h)
-
-    def back_copy(h, t):
+    def sent_in(q):
+        peers(lambda t: sent(outg.at[q, t], in_s.at[q, t]))
+
+    for q in range(QUARTERS):
+        sent_in(q)
+
+    def back_copy(q, t):
         pltpu.make_async_remote_copy(
-            src_ref=outg.at[h, t], dst_ref=ret.at[h, me], send_sem=ret_s.at[h, t], recv_sem=ret_r.at[h, me],
-            device_id=(t, col), device_id_type=MESH,
+            src_ref=outg.at[q, t], dst_ref=ret.at[q, me],
+            send_sem=ret_s.at[q, t], recv_sem=ret_r.at[q, me], device_id=(t, col), device_id_type=MESH,
         ).start()
 
     for g in range(groups):
         if groups > 1:
             far_group(g)
-        pool_grad = nn(far[...], gm[...]).astype(bf16)
-        for h in range(HALVES):
-            outg[h, g * gd : (g + 1) * gd] = pool_grad[:, h * half : (h + 1) * half].reshape(gd, slots, half)
-    for h in range(HALVES):
-        peers(functools.partial(back_copy, h))
-        ret[h, me] = jnp.zeros((slots, half), bf16)
+        pool_grad = nn(jnp.concatenate([far[r] for r in range(BLOCKS)], axis=1), gm[...]).astype(bf16)
+        for q in range(QUARTERS):
+            outg[q, g * gd : (g + 1) * gd] = pool_grad[:, q * quarter : (q + 1) * quarter].reshape(gd, slots, quarter)
+    for q in range(QUARTERS):
+        peers(functools.partial(back_copy, q))
+        ret[q, me] = jnp.zeros((slots, quarter), bf16)
     for k in range(1, depth - 1):
         steps.pop(0)()
         weight_on(0, k)
     for r in range(BLOCKS):
         rs = slice(r * rb, (r + 1) * rb)
-        wide[rs, :] = nn(near[rs, :], gm[...])
+        wide[rs, :] = nn(jnp.concatenate([near[b, rs] for b in range(BLOCKS)], axis=1), gm[...])
     steps.pop(0)()
     weight_on(0, depth - 1)
     weight_on(1, 1)
 
+    for d in range(2, depth):
+        weight_on(1, d)
+
     for h in range(HALVES):
         hs = slice(h * half, (h + 1) * half)
-        peers(lambda s: got(ret.at[h, s], ret_r.at[h, s]))
+        for q in range(h * per_half, (h + 1) * per_half):
+            peers(lambda s: got(ret.at[q, s], ret_r.at[q, s]))
         for g in range(groups):
             if groups > 1:
                 put_selector(g)
-            back = ret[h, g * gd : (g + 1) * gd].reshape(gs, half)
+            back = half_of(ret, h, slice(g * gd, (g + 1) * gd)).reshape(gs, half)
             for r in range(BLOCKS):
                 rs = slice(r * rb, (r + 1) * rb)
                 wide[rs, hs] += tn(sel[:, rs], back)
         ig_out[:, hs] = wide[:, hs].astype(bf16)
 
-    for d in range(2, depth):
-        weight_on(1, d)
     for r in range(BLOCKS):
         piece = act.at[xcol, pl.ds(r * rb, rb)]
         got(piece, ax_r.at[r])
@@ -495,15 +555,15 @@
     got(act.at[pair], ac_r.at[0])
     peers(lambda s: got(brecv.at[s], b_r.at[s]))
     brecv[me] = bsend[...]
-    bg_out[...] = jnp.sum(brecv[...].reshape(n * 8, part), axis=0, keepdims=True)
+    bg_out[...] = jnp.sum(brecv[...], axis=0)
     for r in range(BLOCKS):
         got(act.at[dcol, pl.ds(r * rb, rb)], af_r.at[r])
     for h in range(HALVES):
         weight_end(h)
 
     peers(lambda t: sent(bsend, b_s.at[t]))
-    for h in range(HALVES):
-        peers(lambda t: sent(outg.at[h, t], ret_s.at[h, t]))
+    for q in range(QUARTERS):
+        peers(lambda t: sent(outg.at[q, t], ret_s.at[q, t]))
     for copy in pending:
         copy.wait_send()
 
@@ -539,7 +599,7 @@
     rows, part = features.shape
     width = weight.shape[0]
     slots = send_index.shape[2]
-    half, rb = part // HALVES, rows // BLOCKS
+    half, quarter, rb = part // HALVES, part // QUARTERS, rows // BLOCKS
     gs = min(8, n) * slots
     depth, kb = n // 2, width // n
     edges = local_index.shape[1] + 1 + remote_slot.shape[1]
@@ -548,22 +608,23 @@
     V = pltpu.VMEM
     S = lambda *shape: pltpu.SemaphoreType.DMA(shape)
     buffers = [
-        V((width, part), bf16), V((rows, part), bf16), V((gs, rows), bf16), V((rows, rows), bf16), V((gs, rows), bf16),
+        V((width, part), bf16), V((rows, part), bf16), V((gs, rows), bf16), V((BLOCKS, rows, rb), bf16), V((BLOCKS, gs, rb), bf16),
+        V((rows if n <= 8 else rb, gs), bf16),
         V((edges, 8, rows), i32), V((edges, 8, rows), f32),
-        V((HALVES, n, slots, half), bf16), V((HALVES, n, slots, half), bf16), V((rows, part), f32),
-        V((ncol, HALVES, rows, half), bf16), V((rows, part), bf16),
+        V((QUARTERS, n, slots, quarter), bf16), V((QUARTERS, n, slots, quarter), bf16), V((rows, part), f32),
+        V((ncol, QUARTERS, rows, quarter), bf16), V((rows, part), bf16),
         V((rows, part), f32), V((rows, part), f32),
         V((BLOCKS, 2, rb, part), bf16), V((BLOCKS, 2, rb, part), bf16), V((BLOCKS, rb, part), bf16), V((BLOCKS, rb, part), bf16),
         V((rows, part), bf16), V((width, part), f32),
         *[V((HALVES, depth, kb, half), bf16) for _ in range(5)],
-        V((8, part), f32), V((n, 8, part), f32), V((HALVES, n, slots, half), bf16),
+        V((1, part), f32), V((n, 1, part), f32), V((QUARTERS, n, slots, quarter), bf16),
     ]
     semaphores = [
-        S(2), S(HALVES, n), S(HALVES, n), S(2), S(2),
-        S(HALVES, BLOCKS), S(HALVES, BLOCKS), S(HALVES, BLOCKS), S(HALVES, BLOCKS), S(HALVES, BLOCKS), S(HALVES, BLOCKS),
+        S(2), S(QUARTERS, n), S(QUARTERS, n), S(2, BLOCKS), S(2, BLOCKS),
+        *[S(QUARTERS, BLOCKS) for _ in range(6)],
         S(BLOCKS), S(BLOCKS), S(BLOCKS), S(BLOCKS),
         *[S(HALVES, depth) for _ in range(10)],
-        S(n), S(n), S(HALVES, n), S(HALVES, n),
+        S(n), S(n), S(QUARTERS, n), S(QUARTERS, n),
         S(BLOCKS), S(BLOCKS), S(1), S(1), S(BLOCKS), S(BLOCKS),
     ]
     results = pl.pallas_call(
@@ -582,7 +643,7 @@
         ),
         cost_estimate=pl.CostEstimate(flops=11 << 30, bytes_accessed=16 << 20, transcendentals=1 << 20),
     )(
-        features, weight, layer_bias[None, :], cotangent, self_weight[None, :], local_index.T, local_weight.T,
+        features, weight, layer_bias, cotangent, self_weight[None, :], local_index.T, local_weight.T,
         send_index[0], remote_slot.T, remote_weight.T,
     )
     output, input_grad, weight_grad, bias_grad = pl.pallas_call(

time: 122 us -> 118 us (0.967)
  Pallas kernels: 120 us -> 117 us
  local copies, waits for them, and re-layouts: 1.26 us -> 0 us
    pallas_call x1, Pallas kernels: 115 us -> 113 us  [local(): pl.pallas_call(functools.partial(layer, n=n, ncol=ncol), out_shape=(V((nc...]
    broadcast_in_dim x1 -> x0, local copies, waits for them, and re-layouts: 1.26 us -> none  [local(): layer_bias[None, :]]
where the time goes in v3:
time: 118 us
  Pallas kernels  117 us (99%)
    pallas_call x1, Pallas kernels, local(): pl.pallas_call(functools.partial(layer, n=n, ncol=ncol), out_shape=(V((nc...  113 us
    pallas_call x1, Pallas kernels, local(): pl.pallas_call(store, out_shape=(jax.ShapeDtypeStruct((rows, ncol * part)...  4.32 us

profile of v3, /device:TPU:0, one launch (start us, length us, event | category | flops | bytes accessed | tf_op | source)
XLA Modules:
  0.0 118.0 jit_solution(13091214418002945344)
XLA Ops:
  0.6 112.8 %shard_map.129 = (bf16[4,1024,512]{2,1,0:T(8,128)(2,1)S(1)}, bf16[1024,512]{1,0:T(8,128)(2,1)S(1)}, bf16[2,8,256,256]{3,2,1,0:T(8,128)(2,1)S(1)}, f32[1,512]{1,0:T(1,128)S(1)}) custom-call(bf16[1024,512]{1,0:T(8,128)(2,1)} %feat.1, bf16[2048,512]{1,0:T(8,128)(2,1)} %weight_in.1, bf16[512]{0:T(512)(128)(2,1)} %bias.1, bf16[1024,512]{1,0:T(8,128)(2,1)} %cot_in.1, ...), custom_call_target="tpu_custom_call" | custom-call | flops 11811160064 | bytes 16777216 | tf_op jit(solution)/shard_map/pallas_call | solution.py:630
  113.5 4.3 %shard_map.130 = (bf16[1024,2048]{1,0:T(8,128)(2,1)}, bf16[1024,512]{1,0:T(8,128)(2,1)}, f32[2048,512]{1,0:T(8,128)}, f32[1,512]{1,0:T(1,128)}) custom-call(bf16[4,1024,512]{2,1,0:T(8,128)(2,1)S(1)} %get-tuple-element.12.act, bf16[1024,512]{1,0:T(8,128)(2,1)S(1)} %get-tuple-element.13.ig, bf16[2,8,256,256]{3,2,1,0:T(8,128)(2,1)S(1)} %get-tuple-element.14.wg, ...), custom_call_target="tpu_custom_call" | custom-call | bytes 10485760 | tf_op jit(solution)/shard_map/pallas_call | solution.py:649

commit v4 on v3

--- a/solution.py
+++ b/solution.py
@@ -14,6 +14,7 @@
 BLOCKS = 4
 HALVES = 2
 QUARTERS = 4
+ALONG = QUARTERS - 1
 UNROLL = 8
 ORDER = (
     (0, 0), (0, 1), (1, 0), (1, 1), (0, 2), (1, 2), (2, 0), (2, 1), (2, 2),
@@ -37,7 +38,8 @@
     feat, weight_in, bias, cot_in, selfw, lidx, lwgt, send, ridx, rwgt,
     act, ig_out, wfin, bg_out,
     w_v, cot_v, sel, near, far, turned, edge_pos, edge_w, outg, incg, wide, merged, glow, keep_own, keep_far,
-    csend, crecv, xsend, xrecv, gm, wacc, ysend, yrecv, zsend, from_before, from_after, bsend, brecv, ret,
+    csend, crecv, xsend, xrecv, gm, wacc, ysend, yrecv, zsend, from_before, from_after,
+    pair_send, pair_before, pair_after, bsend, brecv, ret,
     load_s, in_s, in_r, tab_s, tab_r, mx_s, mx_r, mc_s, mc_r, mf_s, mf_r, rc_s, rc_r, rx_s, rx_r,
     y_s, y_r, z_s, fb_r, fa_r, zu_s, zd_s, zg_r, yg_s, yg_r, b_s, b_r, ret_s, ret_r, ax_s, ax_r, ac_s, ac_r, af_s, af_r,
     *, n, ncol,
@@ -331,26 +333,23 @@
     second_half(0)
     total = smooth(0, total)
     cross(2)
+    grads(0)
     second_half(1)
     total = smooth(1, total)
     first_half(3)
     cross(2)
+    grads_over(0)
+    grads(1)
+    cross(1)
     second_half(2)
     total = smooth(2, total)
-    grads(0)
-    cross(1)
     second_half(3)
     total = smooth(3, total)
 
     bsend[...] = jnp.sum(total, axis=0, keepdims=True)
 
-    def cols(h):
-        return slice(h * half, (h + 1) * half)
-
-    def weight_chunk(chunk, h):
-        q, at = lax.div(chunk, HALVES), lax.rem(chunk, HALVES) * per_half
-        rows_in = jnp.concatenate([merged[q, at + p] for p in range(per_half)], axis=1)
-        return tn(rows_in, glow[:, cols(h)])
+    def cols(p):
+        return slice(p * quarter, (p + 1) * quarter)
 
     fine = kb == half
     if not fine:
@@ -358,8 +357,16 @@
             rows_in = half_of(merged.at[chunk // HALVES], chunk % HALVES)
             wacc[chunk * half : (chunk + 1) * half, :] = tn(rows_in, glow[...])
 
-    def block_rows(b):
-        return pl.ds(pl.multiple_of(b * kb, kb), kb)
+    def block_rows(b, count=1):
+        return pl.ds(pl.multiple_of(b * kb, kb), count * kb)
+
+    def weight_chunk(b, h):
+        hs = slice(h * half, (h + 1) * half)
+        if not fine:
+            return wacc[block_rows(b), hs]
+        q, at = lax.div(b, HALVES), lax.rem(b, HALVES) * per_half
+        rows_in = jnp.concatenate([merged[q, at + p] for p in range(per_half)], axis=1)
+        return tn(rows_in, glow[:, hs])
 
     low = zz < depth // 2
     ahead = jnp.where(low, depth - 1 - zz, zz)
@@ -371,106 +378,187 @@
     def weight_out(h, k):
         z = place(k)
         theirs, mine = z * 2 + 1 - yy, z * 2 + yy
+        term = weight_chunk(theirs, h)
+        for p in range(h * per_half, (h + 1) * per_half):
+            piece = term[:, (p - h * per_half) * quarter : (p - h * per_half + 1) * quarter]
+            if p == ALONG:
+                wacc[block_rows(theirs), cols(p)] = piece
+            else:
+                ysend[p, z] = piece.astype(bf16)
+                put(ysend.at[p, z], yrecv.at[p, z], y_s.at[p, z], y_r.at[p, z], ypeer)
         if fine:
-            ysend[h, z] = weight_chunk(theirs, h).astype(bf16)
-        else:
-            ysend[h, z] = wacc[block_rows(theirs), cols(h)].astype(bf16)
-        put(ysend.at[h, z], yrecv.at[h, z], y_s.at[h, z], y_r.at[h, z], ypeer)
-        if fine:
-            wacc[block_rows(mine), cols(h)] = weight_chunk(mine, h)
+            wacc[block_rows(mine), h * half : (h + 1) * half] = weight_chunk(mine, h)
 
     before, after = me - 2, me + 2
 
-    def weight_sum(h, k):
-        z = place(k)
-        got(yrecv.at[h, z], y_r.at[h, z])
-        total = wacc[block_rows(z * 2 + yy), cols(h)] + yrecv[h, z].astype(f32)
-        if k == depth - 1:
-            wacc[block_rows(me), cols(h)] = total
-
+    def line_sum(p, z, total, out, came_before, came_after):
+        out[z] = total.astype(bf16)
+
+        @pl.when(z > zz)
+        def _():
             @pl.when(zz > 0)
             def _():
-                got(from_before.at[h, zz], fb_r.at[h, zz])
-                wacc[block_rows(me), cols(h)] += from_before[h, zz].astype(f32)
-
+                got(came_before.at[z], fb_r.at[p, z])
+                out[z] = (total + came_before[z].astype(f32)).astype(bf16)
+
+            start(out.at[z], came_before.at[z], z_s.at[p, z], fb_r.at[p, z], (after, col))
+
+        @pl.when(z < zz)
+        def _():
             @pl.when(zz < depth - 1)
             def _():
-                got(from_after.at[h, zz], fa_r.at[h, zz])
-                wacc[block_rows(me), cols(h)] += from_after[h, zz].astype(f32)
-
-            wfin[h, me] = wacc[block_rows(me), cols(h)].astype(bf16)
-            weight_share(h, me)
-            return
-        zsend[h, z] = total.astype(bf16)
-
-        @pl.when(z > zz)
-        def _():
-            @pl.when(zz > 0)
-            def _():
-                got(from_before.at[h, z], fb_r.at[h, z])
-                zsend[h, z] = (total + from_before[h, z].astype(f32)).astype(bf16)
-
-            start(zsend.at[h, z], from_before.at[h, z], z_s.at[h, z], fb_r.at[h, z], (after, col))
-
-        @pl.when(z < zz)
-        def _():
-            @pl.when(zz < depth - 1)
-            def _():
-                got(from_after.at[h, z], fa_r.at[h, z])
-                zsend[h, z] = (total + from_after[h, z].astype(f32)).astype(bf16)
-
-            start(zsend.at[h, z], from_after.at[h, z], z_s.at[h, z], fa_r.at[h, z], (before, col))
-
-    def weight_share(h, b, up=True, down=True):
-        z = lax.div(b, 2)
-        block = wfin.at[h, b]
+                got(came_after.at[z], fa_r.at[p, z])
+                out[z] = (total + came_after[z].astype(f32)).astype(bf16)
+
+            start(out.at[z], came_after.at[z], z_s.at[p, z], fa_r.at[p, z], (before, col))
+
+    def line_end(p, rows_in, came_before, came_after):
+        @pl.when(zz > 0)
+        def _():
+            got(came_before.at[zz], fb_r.at[p, zz])
+            wacc[rows_in, cols(p)] += came_before[zz].astype(f32)
+
+        @pl.when(zz < depth - 1)
+        def _():
+            got(came_after.at[zz], fa_r.at[p, zz])
+            wacc[rows_in, cols(p)] += came_after[zz].astype(f32)
+
+    def line_share(p, z, block, up=True, down=True):
         if up:
             @pl.when(zz < depth - 1)
             def _():
-                start(block, block, zu_s.at[h, z], zg_r.at[h, z], (after, col))
+                start(block, block, zu_s.at[p, z], zg_r.at[p, z], (after, col))
         if down:
             @pl.when(zz > 0)
             def _():
-                start(block, block, zd_s.at[h, z], zg_r.at[h, z], (before, col))
-        start(block, block, yg_s.at[h, z], yg_r.at[h, z], ypeer)
-
-    def weight_on(h, d):
+                start(block, block, zd_s.at[p, z], zg_r.at[p, z], (before, col))
+
+    def sent_line(p, z, out, block):
+        @pl.when(z != zz)
+        def _():
+            sent(out.at[z], z_s.at[p, z])
+
+        @pl.when((z <= zz) & (zz < depth - 1))
+        def _():
+            sent(block, zu_s.at[p, z])
+
+        @pl.when((z >= zz) & (zz > 0))
+        def _():
+            sent(block, zd_s.at[p, z])
+
+    def weight_sum(p, k):
+        z = place(k)
+        got(yrecv.at[p, z], y_r.at[p, z])
+        rows_in = block_rows(z * 2 + yy)
+        total = wacc[rows_in, cols(p)] + yrecv[p, z].astype(f32)
+        if k < depth - 1:
+            line_sum(p, z, total, zsend.at[p], from_before.at[p], from_after.at[p])
+            return
+        wacc[rows_in, cols(p)] = total
+        line_end(p, rows_in, from_before.at[p], from_after.at[p])
+        wfin[p, me] = wacc[rows_in, cols(p)].astype(bf16)
+        line_share(p, zz, wfin.at[p, me])
+        across(p, zz)
+
+    def across(p, z):
+        block = wfin.at[p, z * 2 + yy]
+        start(block, block, yg_s.at[p, z], yg_r.at[p, z], ypeer)
+
+    def weight_on(p, d):
         @pl.when(zz >= d)
         def _():
-            got(wfin.at[h, me - 2 * d], zg_r.at[h, zz - d])
-            weight_share(h, me - 2 * d, down=False)
+            block = wfin.at[p, me - 2 * d]
+            got(block, zg_r.at[p, zz - d])
+            line_share(p, zz - d, block, down=False)
+            across(p, zz - d)
 
         @pl.when(zz + d < depth)
         def _():
-            got(wfin.at[h, me + 2 * d], zg_r.at[h, zz + d])
-            weight_share(h, me + 2 * d, up=False)
-
-    def weight_end(h):
+            block = wfin.at[p, me + 2 * d]
+            got(block, zg_r.at[p, zz + d])
+            line_share(p, zz + d, block, up=False)
+            across(p, zz + d)
+
+    def weight_end(p):
         for z in range(depth):
-            got(wfin.at[h, z * 2 + 1 - yy], yg_r.at[h, z])
-            sent(wfin.at[h, z * 2 + yy], yg_s.at[h, z])
-
-            @pl.when(z != zz)
-            def _():
-                sent(zsend.at[h, z], z_s.at[h, z])
-
-            @pl.when((z <= zz) & (zz < depth - 1))
-            def _():
-                sent(wfin.at[h, z * 2 + yy], zu_s.at[h, z])
-
-            @pl.when((z >= zz) & (zz > 0))
-            def _():
-                sent(wfin.at[h, z * 2 + yy], zd_s.at[h, z])
-
-    rest = [functools.partial(weight_out, h, k) for h in range(HALVES) for k in range(depth)]
-    for r in range(1, BLOCKS):
-        rest.pop(0)()
-        grads_over(r - 1)
-        grads(r)
-    rest.pop(0)()
-    grads_over(BLOCKS - 1)
-    for step in rest:
-        step()
+            got(wfin.at[p, z * 2 + 1 - yy], yg_r.at[p, z])
+            sent(wfin.at[p, z * 2 + yy], yg_s.at[p, z])
+            sent_line(p, z, zsend.at[p], wfin.at[p, z * 2 + yy])
+
+    def both(z):
+        return wfin.at[ALONG, pl.ds(z * 2, 2)]
+
+    def along_sum(k):
+        z = place(k)
+        total = wacc[block_rows(z * 2, 2), cols(ALONG)]
+        line_sum(ALONG, z, total, pair_send, pair_before, pair_after)
+
+    end = (zz == 0) | (zz == depth - 1)
+
+    def along_from_end(k):
+        @pl.when(end)
+        def _():
+            along_sum(k)
+
+    def along_inside(k):
+        @pl.when(jnp.logical_not(end))
+        def _():
+            along_sum(k)
+
+    def along_own():
+        line_end(ALONG, block_rows(zz * 2, 2), pair_before, pair_after)
+        ysend[ALONG, zz] = wacc[block_rows(zz * 2 + 1 - yy), cols(ALONG)].astype(bf16)
+        put(ysend.at[ALONG, zz], yrecv.at[ALONG, zz], y_s.at[ALONG, zz], y_r.at[ALONG, zz], ypeer)
+
+    def along_across():
+        got(yrecv.at[ALONG, zz], y_r.at[ALONG, zz])
+        total = wacc[block_rows(me), cols(ALONG)] + yrecv[ALONG, zz].astype(f32)
+        wfin[ALONG, me] = total.astype(bf16)
+        across(ALONG, zz)
+
+    def along_share():
+        got(wfin.at[ALONG, zz * 2 + 1 - yy], yg_r.at[ALONG, zz])
+        line_share(ALONG, zz, both(zz))
+
+    def along_on(d):
+        @pl.when(zz >= d)
+        def _():
+            got(both(zz - d), zg_r.at[ALONG, zz - d])
+            line_share(ALONG, zz - d, both(zz - d), down=False)
+
+        @pl.when(zz + d < depth)
+        def _():
+            got(both(zz + d), zg_r.at[ALONG, zz + d])
+            line_share(ALONG, zz + d, both(zz + d), up=False)
+
+    def along_end():
+        sent(wfin.at[ALONG, me], yg_s.at[ALONG, zz])
+        for z in range(depth):
+            sent_line(ALONG, z, pair_send, both(z))
+
+    def out_along(k):
+        weight_out(HALVES - 1, k)
+        if k < depth - 1:
+            along_from_end(k)
+
+    out_along(0)
+    out_along(1)
+    grads_over(1)
+    grads(2)
+    for k in range(2, depth):
+        out_along(k)
+    weight_out(0, 0)
+    grads_over(2)
+    grads(3)
+    along_inside(0)
+    weight_out(0, 1)
+    grads_over(3)
+    for k in range(1, depth - 2):
+        along_inside(k)
+    for k in range(2, depth):
+        weight_out(0, k)
+    if depth > 2:
+        along_inside(depth - 2)
 
     def bias_copy(t):
         pltpu.make_async_remote_copy(
@@ -487,55 +575,31 @@
     own_act = act.at[col]
     put(own_act, own_act, ac_s.at[0], ac_r.at[0], (me, pair))
 
-    steps = [functools.partial(weight_sum, h, k) for h in range(HALVES) for k in range(depth)]
-    steps.pop(0)()
-    grads_in(0)
-    steps.pop(0)()
-    grads_in(1)
-    for _ in range(depth - 2):
-        steps.pop(0)()
-    grads_in(2)
-    act_over(0)
-    steps.pop(0)()
-    grads_in(3)
-    for r in range(1, BLOCKS):
-        act_over(r)
-
-    def sent_in(q):
-        peers(lambda t: sent(outg.at[q, t], in_s.at[q, t]))
-
-    for q in range(QUARTERS):
-        sent_in(q)
-
     def back_copy(q, t):
         pltpu.make_async_remote_copy(
             src_ref=outg.at[q, t], dst_ref=ret.at[q, me],
             send_sem=ret_s.at[q, t], recv_sem=ret_r.at[q, me], device_id=(t, col), device_id_type=MESH,
         ).start()
 
-    for g in range(groups):
-        if groups > 1:
-            far_group(g)
-        pool_grad = nn(jnp.concatenate([far[r] for r in range(BLOCKS)], axis=1), gm[...]).astype(bf16)
+    def send_back():
         for q in range(QUARTERS):
-            outg[q, g * gd : (g + 1) * gd] = pool_grad[:, q * quarter : (q + 1) * quarter].reshape(gd, slots, quarter)
-    for q in range(QUARTERS):
-        peers(functools.partial(back_copy, q))
-        ret[q, me] = jnp.zeros((slots, quarter), bf16)
-    for k in range(1, depth - 1):
-        steps.pop(0)()
-        weight_on(0, k)
-    for r in range(BLOCKS):
+            peers(lambda t: sent(outg.at[q, t], in_s.at[q, t]))
+        for g in range(groups):
+            if groups > 1:
+                far_group(g)
+            pool_grad = nn(jnp.concatenate([far[r] for r in range(BLOCKS)], axis=1), gm[...]).astype(bf16)
+            for q in range(QUARTERS):
+                piece = pool_grad[:, q * quarter : (q + 1) * quarter]
+                outg[q, g * gd : (g + 1) * gd] = piece.reshape(gd, slots, quarter)
+        for q in range(QUARTERS):
+            peers(functools.partial(back_copy, q))
+            ret[q, me] = jnp.zeros((slots, quarter), bf16)
+
+    def near_back(r):
         rs = slice(r * rb, (r + 1) * rb)
         wide[rs, :] = nn(jnp.concatenate([near[b, rs] for b in range(BLOCKS)], axis=1), gm[...])
-    steps.pop(0)()
-    weight_on(0, depth - 1)
-    weight_on(1, 1)
-
-    for d in range(2, depth):
-        weight_on(1, d)
-
-    for h in range(HALVES):
+
+    def input_grad(h):
         hs = slice(h * half, (h + 1) * half)
         for q in range(h * per_half, (h + 1) * per_half):
             peers(lambda s: got(ret.at[q, s], ret_r.at[q, s]))
@@ -548,18 +612,52 @@
                 wide[rs, hs] += tn(sel[:, rs], back)
         ig_out[:, hs] = wide[:, hs].astype(bf16)
 
-    for r in range(BLOCKS):
+    def act_on(r):
         piece = act.at[xcol, pl.ds(r * rb, rb)]
         got(piece, ax_r.at[r])
         put(piece, piece, af_s.at[r], af_r.at[r], (me, pair))
+
+    events = []
+
+    def at(when, step, *args):
+        events.append((when, len(events), functools.partial(step, *args)))
+
+    unit = 4.0 / depth
+    first, *others = [p for p in reversed(range(QUARTERS)) if p != ALONG]
+    for k in range(depth):
+        last = 2.0 if k == depth - 1 else 0.0
+        at(3.1 + 1.4 * unit * k + last, weight_sum, first, k)
+        for p in others:
+            at(10.5 + 2.8 * unit * k + last, weight_sum, p, k)
+    at(12.0, along_own)
+    at(14.5, along_across)
+    at(17.0, along_share)
+    for d in range(1, depth):
+        at(12.0 + 2.7 * d, weight_on, first, d)
+        at(17.0 + 4.0 * d, along_on, d)
+        for p in others:
+            at(21.5 + 2.8 * d, weight_on, p, d)
+    for r in range(BLOCKS):
+        at(2.6 + 5.7 * r, grads_in, r)
+        at(25.5 + 5.7 * r, act_on, r)
+        at(20.5 + 0.01 * r, near_back, r)
+        at(14.3 if r == 0 else 20.3, act_over, r)
+    at(20.4, send_back)
+    at(36.0, input_grad, 0)
+    at(37.0, input_grad, 1)
+    for _, _, step in sorted(events, key=lambda event: event[:2]):
+        step()
+
     got(act.at[pair], ac_r.at[0])
     peers(lambda s: got(brecv.at[s], b_r.at[s]))
     brecv[me] = bsend[...]
     bg_out[...] = jnp.sum(brecv[...], axis=0)
     for r in range(BLOCKS):
         got(act.at[dcol, pl.ds(r * rb, rb)], af_r.at[r])
-    for h in range(HALVES):
-        weight_end(h)
+    for p in range(QUARTERS):
+        if p != ALONG:
+            weight_end(p)
+    along_end()
 
     peers(lambda t: sent(bsend, b_s.at[t]))
     for q in range(QUARTERS):
@@ -580,11 +678,12 @@
     copies.append(pltpu.make_async_copy(ig, ig_out, some_s.at[ncol]))
     copies[-1].start()
     tall = wide.shape[0] // WRITES
-    group, half = wg.shape[1] // WRITES, wg.shape[3]
+    group, quarter = wg.shape[1] // WRITES, wg.shape[3]
     for p in range(WRITES):
         rs = slice(p * tall, (p + 1) * tall)
-        for h in range(HALVES):
-            wide[rs, h * half : (h + 1) * half] = wg[h, p * group : (p + 1) * group].reshape(tall, half).astype(f32)
+        for c in range(QUARTERS):
+            piece = wg[c, p * group : (p + 1) * group].reshape(tall, quarter)
+            wide[rs, c * quarter : (c + 1) * quarter] = piece.astype(f32)
         copies.append(pltpu.make_async_copy(wide.at[rs], wg_out.at[rs], wg_s.at[p]))
         copies[-1].start()
     bg_out[...] = bg[...]
@@ -616,14 +715,16 @@
         V((rows, part), f32), V((rows, part), f32),
         V((BLOCKS, 2, rb, part), bf16), V((BLOCKS, 2, rb, part), bf16), V((BLOCKS, rb, part), bf16), V((BLOCKS, rb, part), bf16),
         V((rows, part), bf16), V((width, part), f32),
-        *[V((HALVES, depth, kb, half), bf16) for _ in range(5)],
+        *[V((QUARTERS, depth, kb, quarter), bf16) for _ in range(2)],
+        *[V((ALONG, depth, kb, quarter), bf16) for _ in range(3)],
+        *[V((depth, 2 * kb, quarter), bf16) for _ in range(3)],
         V((1, part), f32), V((n, 1, part), f32), V((QUARTERS, n, slots, quarter), bf16),
     ]
     semaphores = [
         S(2), S(QUARTERS, n), S(QUARTERS, n), S(2, BLOCKS), S(2, BLOCKS),
         *[S(QUARTERS, BLOCKS) for _ in range(6)],
         S(BLOCKS), S(BLOCKS), S(BLOCKS), S(BLOCKS),
-        *[S(HALVES, depth) for _ in range(10)],
+        *[S(QUARTERS, depth) for _ in range(10)],
         S(n), S(n), S(QUARTERS, n), S(QUARTERS, n),
         S(BLOCKS), S(BLOCKS), S(1), S(1), S(BLOCKS), S(BLOCKS),
     ]
@@ -632,7 +733,7 @@
         out_shape=(
             V((ncol, rows, part), bf16),
             V((rows, part), bf16),
-            V((HALVES, n, kb, half), bf16),
+            V((QUARTERS, n, kb, quarter), bf16),
             V((1, part), f32),
         ),
         in_specs=[vmem, hbm, vmem, hbm, vmem, vmem, vmem, vmem, vmem, vmem],

time: 118 us -> 115 us (0.975)
  Pallas kernels: 117 us -> 113 us
    pallas_call x1, Pallas kernels: 113 us -> 109 us  [local(): pl.pallas_call(functools.partial(layer, n=n, ncol=ncol), out_shape=(V((nc...]
where the time goes in v4:
time: 115 us; the launch traced here: 114 us
  Pallas kernels  113 us (98%)
    pallas_call x1, Pallas kernels, local(): pl.pallas_call(functools.partial(layer, n=n, ncol=ncol), out_shape=(V((nc...  109 us
    pallas_call x1, Pallas kernels, local(): pl.pallas_call(store, out_shape=(jax.ShapeDtypeStruct((rows, ncol * part)...  4.35 us

profile of v4, /device:TPU:0, one launch (start us, length us, event | category | flops | bytes accessed | tf_op | source)
XLA Modules:
  0.0 114.3 jit_solution(12511587172131835668)
XLA Ops:
  0.6 109.1 %shard_map.129 = (bf16[4,1024,512]{2,1,0:T(8,128)(2,1)S(1)}, bf16[1024,512]{1,0:T(8,128)(2,1)S(1)}, bf16[4,8,256,128]{3,2,1,0:T(8,128)(2,1)S(1)}, f32[1,512]{1,0:T(1,128)S(1)}) custom-call(bf16[1024,512]{1,0:T(8,128)(2,1)} %feat.1, bf16[2048,512]{1,0:T(8,128)(2,1)} %weight_in.1, bf16[512]{0:T(512)(128)(2,1)} %bias.1, bf16[1024,512]{1,0:T(8,128)(2,1)} %cot_in.1, ...), custom_call_target="tpu_custom_call" | custom-call | flops 11811160064 | bytes 16777216 | tf_op jit(solution)/shard_map/pallas_call | solution.py:731
  109.8 4.3 %shard_map.130 = (bf16[1024,2048]{1,0:T(8,128)(2,1)}, bf16[1024,512]{1,0:T(8,128)(2,1)}, f32[2048,512]{1,0:T(8,128)}, f32[1,512]{1,0:T(1,128)}) custom-call(bf16[4,1024,512]{2,1,0:T(8,128)(2,1)S(1)} %get-tuple-element.12.act, bf16[1024,512]{1,0:T(8,128)(2,1)S(1)} %get-tuple-element.13.ig, bf16[4,8,256,128]{3,2,1,0:T(8,128)(2,1)S(1)} %get-tuple-element.14.wg, ...), custom_call_target="tpu_custom_call" | custom-call | bytes 10485760 | tf_op jit(solution)/shard_map/pallas_call | solution.py:750

commit v5 on v4

--- a/solution.py
+++ b/solution.py
@@ -15,6 +15,7 @@
 HALVES = 2
 QUARTERS = 4
 ALONG = QUARTERS - 1
+TIMES = {"in": (0.5, 3.0, 6.0, 10.0, 13.0, 16.0, 18.5, 21.3), "act": 27.0, "near": 21.6, "over": (18.6, 21.4), "back": (13.2, 21.5), "input": (31.0, 37.0)}
 UNROLL = 8
 ORDER = (
     (0, 0), (0, 1), (1, 0), (1, 1), (0, 2), (1, 2), (2, 0), (2, 1), (2, 2),
@@ -35,16 +36,16 @@
 
 
 def layer(
-    feat, weight_in, bias, cot_in, selfw, lidx, lwgt, send, ridx, rwgt,
+    feat_in, weight_in, bias_in, cot_in, selfw_in, lidx_in, lwgt_in, send_in, ridx_in, rwgt_in,
     act, ig_out, wfin, bg_out,
-    w_v, cot_v, sel, near, far, turned, edge_pos, edge_w, outg, incg, wide, merged, glow, keep_own, keep_far,
+    feat, w_v, bias, cot_v, selfw, lidx, lwgt, send, ridx, rwgt, sel, near, far, turned, edge_pos, edge_w, outg, incg, wide, merged, glow, keep_own, keep_far,
     csend, crecv, xsend, xrecv, gm, wacc, ysend, yrecv, zsend, from_before, from_after,
     pair_send, pair_before, pair_after, bsend, brecv, ret,
     load_s, in_s, in_r, tab_s, tab_r, mx_s, mx_r, mc_s, mc_r, mf_s, mf_r, rc_s, rc_r, rx_s, rx_r,
     y_s, y_r, z_s, fb_r, fa_r, zu_s, zd_s, zg_r, yg_s, yg_r, b_s, b_r, ret_s, ret_r, ax_s, ax_r, ac_s, ac_r, af_s, af_r,
     *, n, ncol,
 ):
-    rows, part = feat.shape
+    rows, part = feat_in.shape
     half, quarter = part // HALVES, part // QUARTERS
     per_half = QUARTERS // HALVES
     rb = rows // BLOCKS
@@ -92,14 +93,21 @@
 
         lax.fori_loop(1, n, body, 0)
 
-    load_w = pltpu.make_async_copy(weight_in, w_v, load_s.at[0])
-    load_c = pltpu.make_async_copy(cot_in, cot_v, load_s.at[1])
-    load_w.start()
-    load_c.start()
+    loads = [
+        pltpu.make_async_copy(src, dst, load_s.at[at])
+        for at, (src, dst) in enumerate((
+            (send_in, send), (feat_in, feat), (lidx_in, lidx), (lwgt_in, lwgt), (selfw_in, selfw), (ridx_in, ridx),
+            (rwgt_in, rwgt), (bias_in, bias), (weight_in, w_v), (cot_in, cot_v),
+        ))
+    ]
     barrier = pltpu.get_barrier_semaphore()
     peers(lambda t: pl.semaphore_signal(barrier, inc=1, device_id=(t, col), device_id_type=MESH))
     for other in (pair, xcol):
         pl.semaphore_signal(barrier, inc=1, device_id=(me, other), device_id_type=MESH)
+    for load in loads:
+        load.start()
+    for load in loads[:2]:
+        load.wait()
 
     lane = lax.broadcasted_iota(i32, (slots, rows), 1)
 
@@ -140,6 +148,8 @@
             edge_pos[at + k] = jnp.broadcast_to(idx[k : k + 1, :], (8, rows))
             edge_w[at + k] = jnp.broadcast_to(w[k : k + 1, :], (8, rows))
 
+    for load in loads[2:7]:
+        load.wait()
     put_edges(0, lidx[...], lwgt[...])
     put_edges(local_edges, lax.broadcasted_iota(i32, (1, rows), 1), (1.0 + enhance) * selfw[...])
     put_edges(first_far, ridx[...], rwgt[...])
@@ -250,8 +260,8 @@
         for q, r in ORDER[9:]:
             aggregate(q, r)
 
-    load_w.wait()
-    load_c.wait()
+    for load in loads[7:]:
+        load.wait()
 
     def cross(count):
         for q, r in [crossing.pop(0) for _ in range(count)]:
@@ -313,14 +323,19 @@
     def grads_over(r):
         rs = slice(r * rb, (r + 1) * rb)
         got(crecv.at[r], rc_r.at[r])
-        xsend[r] = (keep_far[rs, :] + crecv[r, 1].astype(f32)).astype(bf16)
-        put(xsend.at[r], xrecv.at[r], rx_s.at[r], rx_r.at[r], (me, xcol))
+        both_halves = (keep_far[rs, :] + crecv[r, 1].astype(f32)).astype(bf16)
+        for h in range(HALVES):
+            xsend[h, r] = both_halves[:, h * half : (h + 1) * half]
+        grads_cross(0, r)
         keep_own[rs, :] += crecv[r, 0].astype(f32)
 
-    def grads_in(r):
-        rs = slice(r * rb, (r + 1) * rb)
-        got(xrecv.at[r], rx_r.at[r])
-        gm[rs, :] = (keep_own[rs, :] + xrecv[r].astype(f32)).astype(bf16)
+    def grads_cross(h, r):
+        put(xsend.at[h, r], xrecv.at[h, r], rx_s.at[h, r], rx_r.at[h, r], (me, xcol))
+
+    def grads_in(h, r):
+        rs, hs = slice(r * rb, (r + 1) * rb), slice(h * half, (h + 1) * half)
+        got(xrecv.at[h, r], rx_r.at[h, r])
+        gm[rs, hs] = (keep_own[rs, hs] + xrecv[h, r].astype(f32)).astype(bf16)
 
     total = jnp.zeros((8, part), f32)
     cross(4)
@@ -339,6 +354,7 @@
     first_half(3)
     cross(2)
     grads_over(0)
+    grads_cross(1, 0)
     grads(1)
     cross(1)
     second_half(2)
@@ -553,6 +569,8 @@
     along_inside(0)
     weight_out(0, 1)
     grads_over(3)
+    for r in range(1, BLOCKS):
+        grads_cross(1, r)
     for k in range(1, depth - 2):
         along_inside(k)
     for k in range(2, depth):
@@ -581,17 +599,19 @@
             send_sem=ret_s.at[q, t], recv_sem=ret_r.at[q, me], device_id=(t, col), device_id_type=MESH,
         ).start()
 
-    def send_back():
-        for q in range(QUARTERS):
+    def send_back(h):
+        quarters = range(h * per_half, (h + 1) * per_half)
+        for q in quarters:
             peers(lambda t: sent(outg.at[q, t], in_s.at[q, t]))
         for g in range(groups):
             if groups > 1:
                 far_group(g)
-            pool_grad = nn(jnp.concatenate([far[r] for r in range(BLOCKS)], axis=1), gm[...]).astype(bf16)
-            for q in range(QUARTERS):
-                piece = pool_grad[:, q * quarter : (q + 1) * quarter]
+            whole = jnp.concatenate([far[r] for r in range(BLOCKS)], axis=1)
+            pool_grad = nn(whole, gm[:, h * half : (h + 1) * half]).astype(bf16)
+            for i, q in enumerate(quarters):
+                piece = pool_grad[:, i * quarter : (i + 1) * quarter]
                 outg[q, g * gd : (g + 1) * gd] = piece.reshape(gd, slots, quarter)
-        for q in range(QUARTERS):
+        for q in quarters:
             peers(functools.partial(back_copy, q))
             ret[q, me] = jnp.zeros((slots, quarter), bf16)
 
@@ -637,14 +657,16 @@
         at(17.0 + 4.0 * d, along_on, d)
         for p in others:
             at(21.5 + 2.8 * d, weight_on, p, d)
+    crossed = ((0, 0), (1, 0), (0, 1), (0, 2), (0, 3), (1, 1), (1, 2), (1, 3))
+    for when, (h, r) in zip(TIMES["in"], crossed):
+        at(when, grads_in, h, r)
     for r in range(BLOCKS):
-        at(2.6 + 5.7 * r, grads_in, r)
-        at(25.5 + 5.7 * r, act_on, r)
-        at(20.5 + 0.01 * r, near_back, r)
-        at(14.3 if r == 0 else 20.3, act_over, r)
-    at(20.4, send_back)
-    at(36.0, input_grad, 0)
-    at(37.0, input_grad, 1)
+        at(TIMES["act"] + 5.7 * r, act_on, r)
+        at(TIMES["near"] + 0.01 * r, near_back, r)
+        at(TIMES["over"][0 if r == 0 else 1], act_over, r)
+    for h in range(HALVES):
+        at(TIMES["back"][h], send_back, h)
+        at(TIMES["input"][h], input_grad, h)
     for _, _, step in sorted(events, key=lambda event: event[:2]):
         step()
 
@@ -701,19 +723,22 @@
     half, quarter, rb = part // HALVES, part // QUARTERS, rows // BLOCKS
     gs = min(8, n) * slots
     depth, kb = n // 2, width // n
-    edges = local_index.shape[1] + 1 + remote_slot.shape[1]
+    edges_near, edges_far = local_index.shape[1], remote_slot.shape[1]
+    edges = edges_near + 1 + edges_far
     vmem = pl.BlockSpec(memory_space=pltpu.VMEM)
     hbm = pl.BlockSpec(memory_space=pl.ANY)
     V = pltpu.VMEM
     S = lambda *shape: pltpu.SemaphoreType.DMA(shape)
     buffers = [
-        V((width, part), bf16), V((rows, part), bf16), V((gs, rows), bf16), V((BLOCKS, rows, rb), bf16), V((BLOCKS, gs, rb), bf16),
+        V((rows, part), bf16), V((width, part), bf16), V((part,), bf16), V((rows, part), bf16), V((1, rows), f32),
+        V((edges_near, rows), i32), V((edges_near, rows), f32), V((n, slots), i32), V((edges_far, rows), i32), V((edges_far, rows), f32),
+        V((gs, rows), bf16), V((BLOCKS, rows, rb), bf16), V((BLOCKS, gs, rb), bf16),
         V((rows if n <= 8 else rb, gs), bf16),
         V((edges, 8, rows), i32), V((edges, 8, rows), f32),
         V((QUARTERS, n, slots, quarter), bf16), V((QUARTERS, n, slots, quarter), bf16), V((rows, part), f32),
         V((ncol, QUARTERS, rows, quarter), bf16), V((rows, part), bf16),
         V((rows, part), f32), V((rows, part), f32),
-        V((BLOCKS, 2, rb, part), bf16), V((BLOCKS, 2, rb, part), bf16), V((BLOCKS, rb, part), bf16), V((BLOCKS, rb, part), bf16),
+        V((BLOCKS, 2, rb, part), bf16), V((BLOCKS, 2, rb, part), bf16), *[V((HALVES, BLOCKS, rb, half), bf16) for _ in range(2)],
         V((rows, part), bf16), V((width, part), f32),
         *[V((QUARTERS, depth, kb, quarter), bf16) for _ in range(2)],
         *[V((ALONG, depth, kb, quarter), bf16) for _ in range(3)],
@@ -721,9 +746,9 @@
         V((1, part), f32), V((n, 1, part), f32), V((QUARTERS, n, slots, quarter), bf16),
     ]
     semaphores = [
-        S(2), S(QUARTERS, n), S(QUARTERS, n), S(2, BLOCKS), S(2, BLOCKS),
+        S(10), S(QUARTERS, n), S(QUARTERS, n), S(2, BLOCKS), S(2, BLOCKS),
         *[S(QUARTERS, BLOCKS) for _ in range(6)],
-        S(BLOCKS), S(BLOCKS), S(BLOCKS), S(BLOCKS),
+        S(BLOCKS), S(BLOCKS), S(HALVES, BLOCKS), S(HALVES, BLOCKS),
         *[S(QUARTERS, depth) for _ in range(10)],
         S(n), S(n), S(QUARTERS, n), S(QUARTERS, n),
         S(BLOCKS), S(BLOCKS), S(1), S(1), S(BLOCKS), S(BLOCKS),
@@ -736,7 +761,7 @@
             V((QUARTERS, n, kb, quarter), bf16),
             V((1, part), f32),
         ),
-        in_specs=[vmem, hbm, vmem, hbm, vmem, vmem, vmem, vmem, vmem, vmem],
+        in_specs=[hbm] * 10,
         out_specs=(vmem,) * 4,
         scratch_shapes=buffers + semaphores,
         compiler_params=pltpu.CompilerParams(

time: 115 us -> 113 us (0.983)
    pallas_call x1, Pallas kernels: 109 us -> 108 us  [local(): pl.pallas_call(functools.partial(layer, n=n, ncol=ncol), out_shape=(V((nc...]
where the time goes in v5:
time: 113 us
  Pallas kernels  112 us (99%)
    pallas_call x1, Pallas kernels, local(): pl.pallas_call(functools.partial(layer, n=n, ncol=ncol), out_shape=(V((nc...  108 us
    pallas_call x1, Pallas kernels, local(): pl.pallas_call(store, out_shape=(jax.ShapeDtypeStruct((rows, ncol * part)...  4.35 us

profile of v5, /device:TPU:0, one launch (start us, length us, event | category | flops | bytes accessed | tf_op | source)
XLA Modules:
  0.0 112.7 jit_solution(15586395002412968322)
XLA Ops:
  0.6 107.6 %shard_map.129 = (bf16[4,1024,512]{2,1,0:T(8,128)(2,1)S(1)}, bf16[1024,512]{1,0:T(8,128)(2,1)S(1)}, bf16[4,8,256,128]{3,2,1,0:T(8,128)(2,1)S(1)}, f32[1,512]{1,0:T(1,128)S(1)}) custom-call(bf16[1024,512]{1,0:T(8,128)(2,1)} %feat_in.1, bf16[2048,512]{1,0:T(8,128)(2,1)} %weight_in.1, bf16[512]{0:T(512)(128)(2,1)} %bias_in.1, bf16[1024,512]{1,0:T(8,128)(2,1)} %cot_in.1, ...), custom_call_target="tpu_custom_call" | custom-call | flops 11811160064 | bytes 16777216 | tf_op jit(solution)/shard_map/pallas_call | solution.py:756
  108.2 4.3 %shard_map.130 = (bf16[1024,2048]{1,0:T(8,128)(2,1)}, bf16[1024,512]{1,0:T(8,128)(2,1)}, f32[2048,512]{1,0:T(8,128)}, f32[1,512]{1,0:T(1,128)}) custom-call(bf16[4,1024,512]{2,1,0:T(8,128)(2,1)S(1)} %get-tuple-element.12.act, bf16[1024,512]{1,0:T(8,128)(2,1)S(1)} %get-tuple-element.13.ig, bf16[4,8,256,128]{3,2,1,0:T(8,128)(2,1)S(1)} %get-tuple-element.14.wg, ...), custom_call_target="tpu_custom_call" | custom-call | bytes 10485760 | tf_op jit(solution)/shard_map/pallas_call | solution.py:775

commit v6 on v5

--- a/solution.py
+++ b/solution.py
@@ -14,8 +14,8 @@
 BLOCKS = 4
 HALVES = 2
 QUARTERS = 4
-ALONG = QUARTERS - 1
-TIMES = {"in": (0.5, 3.0, 6.0, 10.0, 13.0, 16.0, 18.5, 21.3), "act": 27.0, "near": 21.6, "over": (18.6, 21.4), "back": (13.2, 21.5), "input": (31.0, 37.0)}
+PIECES = (3, 2, 1, 0)
+TIMES = {"sum": 3.8, "own": 2.0, "on": 17.5, "hop": 3.3, "in": (0.5, 3.0, 6.0, 10.0, 13.0, 16.0, 18.5, 21.3), "act": 27.0, "near": 21.6, "over": (18.6, 21.4), "back": (13.2, 21.5), "input": (31.0, 37.0)}
 UNROLL = 8
 ORDER = (
     (0, 0), (0, 1), (1, 0), (1, 1), (0, 2), (1, 2), (2, 0), (2, 1), (2, 2),
@@ -39,8 +39,7 @@
     feat_in, weight_in, bias_in, cot_in, selfw_in, lidx_in, lwgt_in, send_in, ridx_in, rwgt_in,
     act, ig_out, wfin, bg_out,
     feat, w_v, bias, cot_v, selfw, lidx, lwgt, send, ridx, rwgt, sel, near, far, turned, edge_pos, edge_w, outg, incg, wide, merged, glow, keep_own, keep_far,
-    csend, crecv, xsend, xrecv, gm, wacc, ysend, yrecv, zsend, from_before, from_after,
-    pair_send, pair_before, pair_after, bsend, brecv, ret,
+    csend, crecv, xsend, xrecv, gm, wacc, ysend, yrecv, zsend, from_before, from_after, bsend, brecv, ret,
     load_s, in_s, in_r, tab_s, tab_r, mx_s, mx_r, mc_s, mc_r, mf_s, mf_r, rc_s, rc_r, rx_s, rx_r,
     y_s, y_r, z_s, fb_r, fa_r, zu_s, zd_s, zg_r, yg_s, yg_r, b_s, b_r, ret_s, ret_r, ax_s, ax_r, ac_s, ac_r, af_s, af_r,
     *, n, ncol,
@@ -397,11 +396,8 @@
         term = weight_chunk(theirs, h)
         for p in range(h * per_half, (h + 1) * per_half):
             piece = term[:, (p - h * per_half) * quarter : (p - h * per_half + 1) * quarter]
-            if p == ALONG:
-                wacc[block_rows(theirs), cols(p)] = piece
-            else:
-                ysend[p, z] = piece.astype(bf16)
-                put(ysend.at[p, z], yrecv.at[p, z], y_s.at[p, z], y_r.at[p, z], ypeer)
+            ysend[p, z] = piece.astype(bf16)
+            put(ysend.at[p, z], yrecv.at[p, z], y_s.at[p, z], y_r.at[p, z], ypeer)
         if fine:
             wacc[block_rows(mine), h * half : (h + 1) * half] = weight_chunk(mine, h)
 
@@ -501,82 +497,20 @@
             sent(wfin.at[p, z * 2 + yy], yg_s.at[p, z])
             sent_line(p, z, zsend.at[p], wfin.at[p, z * 2 + yy])
 
-    def both(z):
-        return wfin.at[ALONG, pl.ds(z * 2, 2)]
-
-    def along_sum(k):
-        z = place(k)
-        total = wacc[block_rows(z * 2, 2), cols(ALONG)]
-        line_sum(ALONG, z, total, pair_send, pair_before, pair_after)
-
-    end = (zz == 0) | (zz == depth - 1)
-
-    def along_from_end(k):
-        @pl.when(end)
-        def _():
-            along_sum(k)
-
-    def along_inside(k):
-        @pl.when(jnp.logical_not(end))
-        def _():
-            along_sum(k)
-
-    def along_own():
-        line_end(ALONG, block_rows(zz * 2, 2), pair_before, pair_after)
-        ysend[ALONG, zz] = wacc[block_rows(zz * 2 + 1 - yy), cols(ALONG)].astype(bf16)
-        put(ysend.at[ALONG, zz], yrecv.at[ALONG, zz], y_s.at[ALONG, zz], y_r.at[ALONG, zz], ypeer)
-
-    def along_across():
-        got(yrecv.at[ALONG, zz], y_r.at[ALONG, zz])
-        total = wacc[block_rows(me), cols(ALONG)] + yrecv[ALONG, zz].astype(f32)
-        wfin[ALONG, me] = total.astype(bf16)
-        across(ALONG, zz)
-
-    def along_share():
-        got(wfin.at[ALONG, zz * 2 + 1 - yy], yg_r.at[ALONG, zz])
-        line_share(ALONG, zz, both(zz))
-
-    def along_on(d):
-        @pl.when(zz >= d)
-        def _():
-            got(both(zz - d), zg_r.at[ALONG, zz - d])
-            line_share(ALONG, zz - d, both(zz - d), down=False)
-
-        @pl.when(zz + d < depth)
-        def _():
-            got(both(zz + d), zg_r.at[ALONG, zz + d])
-            line_share(ALONG, zz + d, both(zz + d), up=False)
-
-    def along_end():
-        sent(wfin.at[ALONG, me], yg_s.at[ALONG, zz])
-        for z in range(depth):
-            sent_line(ALONG, z, pair_send, both(z))
-
-    def out_along(k):
+    for k in range(depth):
         weight_out(HALVES - 1, k)
-        if k < depth - 1:
-            along_from_end(k)
-
-    out_along(0)
-    out_along(1)
-    grads_over(1)
-    grads(2)
-    for k in range(2, depth):
-        out_along(k)
+        if k == 1:
+            grads_over(1)
+            grads(2)
     weight_out(0, 0)
     grads_over(2)
     grads(3)
-    along_inside(0)
     weight_out(0, 1)
     grads_over(3)
+    for k in range(2, depth):
+        weight_out(0, k)
     for r in range(1, BLOCKS):
         grads_cross(1, r)
-    for k in range(1, depth - 2):
-        along_inside(k)
-    for k in range(2, depth):
-        weight_out(0, k)
-    if depth > 2:
-        along_inside(depth - 2)
 
     def bias_copy(t):
         pltpu.make_async_remote_copy(
@@ -643,20 +577,12 @@
         events.append((when, len(events), functools.partial(step, *args)))
 
     unit = 4.0 / depth
-    first, *others = [p for p in reversed(range(QUARTERS)) if p != ALONG]
     for k in range(depth):
-        last = 2.0 if k == depth - 1 else 0.0
-        at(3.1 + 1.4 * unit * k + last, weight_sum, first, k)
-        for p in others:
-            at(10.5 + 2.8 * unit * k + last, weight_sum, p, k)
-    at(12.0, along_own)
-    at(14.5, along_across)
-    at(17.0, along_share)
+        for i, p in enumerate(PIECES):
+            at(TIMES["sum"] + 11.2 * (i // 2) + 2.8 * unit * k + (TIMES["own"] if k == depth - 1 else 0.0), weight_sum, p, k)
     for d in range(1, depth):
-        at(12.0 + 2.7 * d, weight_on, first, d)
-        at(17.0 + 4.0 * d, along_on, d)
-        for p in others:
-            at(21.5 + 2.8 * d, weight_on, p, d)
+        for i, p in enumerate(PIECES):
+            at(TIMES["on"] + 11.2 * (i // 2) + TIMES["hop"] * d, weight_on, p, d)
     crossed = ((0, 0), (1, 0), (0, 1), (0, 2), (0, 3), (1, 1), (1, 2), (1, 3))
     for when, (h, r) in zip(TIMES["in"], crossed):
         at(when, grads_in, h, r)
@@ -676,10 +602,8 @@
     bg_out[...] = jnp.sum(brecv[...], axis=0)
     for r in range(BLOCKS):
         got(act.at[dcol, pl.ds(r * rb, rb)], af_r.at[r])
-    for p in range(QUARTERS):
-        if p != ALONG:
-            weight_end(p)
-    along_end()
+    for p in PIECES:
+        weight_end(p)
 
     peers(lambda t: sent(bsend, b_s.at[t]))
     for q in range(QUARTERS):
@@ -741,8 +665,7 @@
         V((BLOCKS, 2, rb, part), bf16), V((BLOCKS, 2, rb, part), bf16), *[V((HALVES, BLOCKS, rb, half), bf16) for _ in range(2)],
         V((rows, part), bf16), V((width, part), f32),
         *[V((QUARTERS, depth, kb, quarter), bf16) for _ in range(2)],
-        *[V((ALONG, depth, kb, quarter), bf16) for _ in range(3)],
-        *[V((depth, 2 * kb, quarter), bf16) for _ in range(3)],
+        *[V((len(PIECES), depth, kb, quarter), bf16) for _ in range(3)],
         V((1, part), f32), V((n, 1, part), f32), V((QUARTERS, n, slots, quarter), bf16),
     ]
     semaphores = [

time: 113 us -> 108 us (0.956)
  Pallas kernels: 112 us -> 107 us
    pallas_call x1, Pallas kernels: 108 us -> 102 us  [local(): pl.pallas_call(functools.partial(layer, n=n, ncol=ncol), out_shape=(V((nc...]
where the time goes in v6:
time: 108 us; the launch traced here: 107 us
  Pallas kernels  107 us (99%)
    pallas_call x1, Pallas kernels, local(): pl.pallas_call(functools.partial(layer, n=n, ncol=ncol), out_shape=(V((nc...  102 us
    pallas_call x1, Pallas kernels, local(): pl.pallas_call(store, out_shape=(jax.ShapeDtypeStruct((rows, ncol * part)...  4.35 us

profile of v6, /device:TPU:0, one launch (start us, length us, event | category | flops | bytes accessed | tf_op | source)
XLA Modules:
  0.0 107.5 jit_solution(2582421913163824011)
XLA Ops:
  0.6 102.3 %shard_map.129 = (bf16[4,1024,512]{2,1,0:T(8,128)(2,1)S(1)}, bf16[1024,512]{1,0:T(8,128)(2,1)S(1)}, bf16[4,8,256,128]{3,2,1,0:T(8,128)(2,1)S(1)}, f32[1,512]{1,0:T(1,128)S(1)}) custom-call(bf16[1024,512]{1,0:T(8,128)(2,1)} %feat_in.1, bf16[2048,512]{1,0:T(8,128)(2,1)} %weight_in.1, bf16[512]{0:T(512)(128)(2,1)} %bias_in.1, bf16[1024,512]{1,0:T(8,128)(2,1)} %cot_in.1, ...), custom_call_target="tpu_custom_call" | custom-call | flops 11811160064 | bytes 16777216 | tf_op jit(solution)/shard_map/pallas_call | solution.py:679
  103.0 4.3 %shard_map.130 = (bf16[1024,2048]{1,0:T(8,128)(2,1)}, bf16[1024,512]{1,0:T(8,128)(2,1)}, f32[2048,512]{1,0:T(8,128)}, f32[1,512]{1,0:T(1,128)}) custom-call(bf16[4,1024,512]{2,1,0:T(8,128)(2,1)S(1)} %get-tuple-element.12.act, bf16[1024,512]{1,0:T(8,128)(2,1)S(1)} %get-tuple-element.13.ig, bf16[4,8,256,128]{3,2,1,0:T(8,128)(2,1)S(1)} %get-tuple-element.14.wg, ...), custom_call_target="tpu_custom_call" | custom-call | bytes 10485760 | tf_op jit(solution)/shard_map/pallas_call | solution.py:698

commit v7 on v6

--- a/solution.py
+++ b/solution.py
@@ -15,7 +15,7 @@
 HALVES = 2
 QUARTERS = 4
 PIECES = (3, 2, 1, 0)
-TIMES = {"sum": 3.8, "own": 2.0, "on": 17.5, "hop": 3.3, "in": (0.5, 3.0, 6.0, 10.0, 13.0, 16.0, 18.5, 21.3), "act": 27.0, "near": 21.6, "over": (18.6, 21.4), "back": (13.2, 21.5), "input": (31.0, 37.0)}
+TIMES = {"sum": 3.8, "own": 2.0, "on": (17.5, 26.5), "hop": 3.3, "in": (0.5, 3.0, 6.0, 10.0, 13.0, 16.0, 18.5, 21.3), "act": 27.0, "near": 21.6, "over": (18.6, 21.4), "back": (13.2, 21.5), "input": (31.0, 37.0)}
 UNROLL = 8
 ORDER = (
     (0, 0), (0, 1), (1, 0), (1, 1), (0, 2), (1, 2), (2, 0), (2, 1), (2, 2),
@@ -582,7 +582,7 @@
             at(TIMES["sum"] + 11.2 * (i // 2) + 2.8 * unit * k + (TIMES["own"] if k == depth - 1 else 0.0), weight_sum, p, k)
     for d in range(1, depth):
         for i, p in enumerate(PIECES):
-            at(TIMES["on"] + 11.2 * (i // 2) + TIMES["hop"] * d, weight_on, p, d)
+            at(TIMES["on"][i // 2] + TIMES["hop"] * d, weight_on, p, d)
     crossed = ((0, 0), (1, 0), (0, 1), (0, 2), (0, 3), (1, 1), (1, 2), (1, 3))
     for when, (h, r) in zip(TIMES["in"], crossed):
         at(when, grads_in, h, r)
@@ -618,10 +618,14 @@
 def store(act, ig, wg, bg, act_out, ig_out, wg_out, bg_out, wide, some_s, wg_s):
     ncol, part = act.shape[0], act.shape[2]
     copies = []
-    for q in range(ncol):
-        copies.append(pltpu.make_async_copy(act.at[q], act_out.at[:, q * part : (q + 1) * part], some_s.at[q]))
-        copies[-1].start()
-    copies.append(pltpu.make_async_copy(ig, ig_out, some_s.at[ncol]))
+    rb = act.shape[1] // BLOCKS
+    for r in range(BLOCKS):
+        rs = slice(r * rb, (r + 1) * rb)
+        for q in range(ncol):
+            out = act_out.at[rs, q * part : (q + 1) * part]
+            copies.append(pltpu.make_async_copy(act.at[q, rs], out, some_s.at[r * ncol + q]))
+            copies[-1].start()
+    copies.append(pltpu.make_async_copy(ig, ig_out, some_s.at[BLOCKS * ncol]))
     copies[-1].start()
     tall = wide.shape[0] // WRITES
     group, quarter = wg.shape[1] // WRITES, wg.shape[3]
@@ -705,7 +709,7 @@
         ),
         in_specs=[vmem] * 4,
         out_specs=(hbm, hbm, hbm, vmem),
-        scratch_shapes=[V((width, part), f32), S(ncol + 1), S(WRITES)],
+        scratch_shapes=[V((width, part), f32), S(BLOCKS * ncol + 1), S(WRITES)],
         compiler_params=pltpu.CompilerParams(vmem_limit_bytes=6 << 20),
         cost_estimate=pl.CostEstimate(flops=0, bytes_accessed=10 << 20, transcendentals=0),
     )(*results)

time: 108 us -> 108 us (level)
  no operation moved by 1% of the time
where the time goes in v7:
time: 108 us
  Pallas kernels  107 us (99%)
    pallas_call x1, Pallas kernels, local(): pl.pallas_call(functools.partial(layer, n=n, ncol=ncol), out_shape=(V((nc...  102 us
    pallas_call x1, Pallas kernels, local(): pl.pallas_call(store, out_shape=(jax.ShapeDtypeStruct((rows, ncol * part)...  4.39 us

profile of v7, /device:TPU:0, one launch (start us, length us, event | category | flops | bytes accessed | tf_op | source)
XLA Modules:
  0.0 107.5 jit_solution(17349008315898994370)
XLA Ops:
  0.6 102.3 %shard_map.129 = (bf16[4,1024,512]{2,1,0:T(8,128)(2,1)S(1)}, bf16[1024,512]{1,0:T(8,128)(2,1)S(1)}, bf16[4,8,256,128]{3,2,1,0:T(8,128)(2,1)S(1)}, f32[1,512]{1,0:T(1,128)S(1)}) custom-call(bf16[1024,512]{1,0:T(8,128)(2,1)} %feat_in.1, bf16[2048,512]{1,0:T(8,128)(2,1)} %weight_in.1, bf16[512]{0:T(512)(128)(2,1)} %bias_in.1, bf16[1024,512]{1,0:T(8,128)(2,1)} %cot_in.1, ...), custom_call_target="tpu_custom_call" | custom-call | flops 11811160064 | bytes 16777216 | tf_op jit(solution)/shard_map/pallas_call | solution.py:683
  103.0 4.4 %shard_map.130 = (bf16[1024,2048]{1,0:T(8,128)(2,1)}, bf16[1024,512]{1,0:T(8,128)(2,1)}, f32[2048,512]{1,0:T(8,128)}, f32[1,512]{1,0:T(1,128)}) custom-call(bf16[4,1024,512]{2,1,0:T(8,128)(2,1)S(1)} %get-tuple-element.12.act, bf16[1024,512]{1,0:T(8,128)(2,1)S(1)} %get-tuple-element.13.ig, bf16[4,8,256,128]{3,2,1,0:T(8,128)(2,1)S(1)} %get-tuple-element.14.wg, ...), custom_call_target="tpu_custom_call" | custom-call | bytes 10485760 | tf_op jit(solution)/shard_map/pallas_call | solution.py:702
